TPU v7x, 512 devices: a whole 4x8x8 slice. The times are simulated.
512 devices in a mesh: rows: 64 (over x, y, core), cols: 8 (over z).
Axes of the slice: x: 4, y: 8, z: 8, core: 2. Of those that a mesh axis runs over, the one named last changes fastest.
Arguments:
- data: float32 [80, 32768], P(None, 'rows'), may hold values from -6 to 6
- source: int32 [32768], P('rows'), may hold values from 0 to 32767, as said below
- near_tiles: bfloat16 [1920, 1024, 512], P('rows', 'cols'), may hold values from -0.046875 to 0.046875
- near_rows: int32 [1920, 8], P('rows', 'cols'), may hold values from 0 to 3, as said below
- near_cols: int32 [1920, 8], P('rows', 'cols'), may hold values from 0 to 9, as said below
- near_count: int32 [64, 8], P('rows', 'cols'), may hold values from 0 to 30, as said below
- far_left: bfloat16 [192, 32768], P('cols', 'rows'), may hold values from -0.4375 to 0.4375
- far_right: bfloat16 [1536, 40960], P('rows', 'cols'), may hold values from -0.078125 to 0.078125
Outputs:
- slip: float32 [80, 40960], P(None, ('cols', 'rows'))
- misfit: float32 [80, 32768], P(None, 'rows')
Inputs may be any that keep to these rules, and one draw needn't show every extreme that they name: source is a permutation of the pixels; the burst position source[j] lies in the cluster of pixel j or in one of the two clusters beside it, counted cyclically. The slots of one cluster pair name distinct pairs of sub-clusters (near_rows, near_cols). `near_cols`: see near_rows. Slots at or beyond near_count are ignored; near_count[r, c] is zero unless c is the patch cluster adjacent to pixel cluster r (r times the number of patch clusters over the number of pixel clusters, rounded down) or the next one after it, counted cyclically; there it is 7 or more.
All inputs are finite; a program needn't handle non-finite values.
Results may differ from a plain program's by a relative error of at most 0.02.
Values may be sent and summed in bfloat16 or wider, within the bound.
A program may use at most 64 MiB of HBM per device.

v0:
```python
import jax
import jax.numpy as jnp
from jax import lax
from jax.sharding import PartitionSpec as P

ITERS = 2


EPSILON = 1e-06


def with_halo(block, sides, width):
    for axis, dim in sides:
        count = lax.axis_size(axis)
        forward = [(i, i + 1) for i in range(count - 1)]
        forward.append((count - 1, 0))
        backward = [(target, source) for source, target in forward]
        low = lax.ppermute(
            lax.slice_in_dim(block, block.shape[dim] - width, None, axis=dim), axis, forward
        )
        high = lax.ppermute(lax.slice_in_dim(block, 0, width, axis=dim), axis, backward)
        block = jnp.concatenate([low, block, high], axis=dim)
    return block


def far_forward(vector_b, far_left, far_right):
    inner = jnp.dot(vector_b, far_right.T, preferred_element_type=jnp.float32).astype(jnp.bfloat16)
    return jnp.dot(inner, far_left, preferred_element_type=jnp.float32)


def far_adjoint(pixel_b, far_left, far_right):
    outer = jnp.dot(pixel_b, far_left.T, preferred_element_type=jnp.float32).astype(jnp.bfloat16)
    return jnp.dot(outer, far_right, preferred_element_type=jnp.float32)


def padded_forward(vector_b, tiles, rows_index, cols_index, count, pixels):
    realiz, width = vector_b.shape
    slots, tile_rows, tile_cols = tiles.shape
    pieces = jnp.take(vector_b.reshape(realiz, width // tile_cols, tile_cols), cols_index, axis=1)
    products = jnp.einsum("knq,npq->nkp", pieces, tiles, preferred_element_type=jnp.float32)
    live = (jnp.arange(slots) < count).astype(jnp.float32)
    placing = (rows_index[:, None] == jnp.arange(pixels // tile_rows)[None, :]).astype(
        jnp.float32
    ) * live[:, None]
    return jnp.einsum("nkp,na->kap", products, placing).reshape(realiz, pixels)


def padded_adjoint(pixel_b, tiles, rows_index, cols_index, count, width):
    realiz, pixels = pixel_b.shape
    slots, tile_rows, tile_cols = tiles.shape
    pieces = jnp.take(pixel_b.reshape(realiz, pixels // tile_rows, tile_rows), rows_index, axis=1)
    products = jnp.einsum("knp,npq->nkq", pieces, tiles, preferred_element_type=jnp.float32)
    live = (jnp.arange(slots) < count).astype(jnp.float32)
    placing = (cols_index[:, None] == jnp.arange(width // tile_cols)[None, :]).astype(
        jnp.float32
    ) * live[:, None]
    return jnp.einsum("nkq,nb->kbq", products, placing).reshape(realiz, width)


def body(data, source, near_tiles, near_rows, near_cols, near_count, far_left, far_right):
    pixels = data.shape[1]
    width = far_right.shape[1]
    rows_total = lax.axis_size("rows")
    row_place = lax.axis_index("rows")
    rows_index = near_rows.reshape(-1)
    cols_index = near_cols.reshape(-1)
    count = near_count[0, 0]
    share = width // rows_total
    extended = with_halo(data, (("rows", 1),), pixels)
    offsets = (source - (row_place - 1) * pixels + rows_total * pixels) % (rows_total * pixels)
    observed = jnp.take(extended, offsets, axis=1)

    def apply_forward(vector_b):
        near_term = padded_forward(vector_b, near_tiles, rows_index, cols_index, count, pixels)
        return lax.psum(
            (far_forward(vector_b, far_left, far_right) + near_term).astype(jnp.bfloat16), "cols"
        ).astype(jnp.float32)

    def apply_adjoint(pixel_b):
        near_term = padded_adjoint(pixel_b, near_tiles, rows_index, cols_index, count, width)
        return far_adjoint(pixel_b, far_left, far_right) + near_term

    def pixel_norm(field):
        return jnp.sqrt(lax.psum(jnp.sum(field * field, axis=1), "rows") + EPSILON)

    def slip_update(partial_value, beta_now, previous):
        summed = lax.psum(partial_value, "rows")
        if previous is not None:
            summed = summed - beta_now[:, None] * previous
        squares = lax.psum(jnp.sum(summed * summed, axis=1), "cols")
        alpha_now = jnp.sqrt(squares + EPSILON)
        return (summed / alpha_now[:, None], alpha_now)

    def for_products(field):
        return field.astype(jnp.bfloat16)

    beta = pixel_norm(observed)
    left = observed / beta[:, None]
    right, alpha = slip_update(apply_adjoint(left.astype(jnp.bfloat16)), beta, None)
    direction = right
    solution = jnp.zeros_like(right)
    phibar = beta
    rhobar = alpha
    for step in range(ITERS):
        left = apply_forward(for_products(right)) - alpha[:, None] * left
        beta = pixel_norm(left)
        left = left / beta[:, None]
        rho = jnp.sqrt(rhobar * rhobar + beta * beta)
        cosine = rhobar / rho
        sine = beta / rho
        phi = cosine * phibar
        phibar = sine * phibar
        solution = solution + (phi / rho)[:, None] * direction
        if step + 1 < ITERS:
            right, alpha = slip_update(apply_adjoint(left.astype(jnp.bfloat16)), beta, right)
            theta = sine * alpha
            rhobar = -cosine * alpha
            direction = right - (theta / rho)[:, None] * direction
    misfit = observed - apply_forward(for_products(solution))
    return (lax.dynamic_slice_in_dim(solution, row_place * share, share, 1), misfit)


def solution(mesh):
    return jax.shard_map(
        body,
        mesh=mesh,
        in_specs=(
            P(None, "rows"),
            P("rows"),
            P("rows", "cols", None),
            P("rows", "cols"),
            P("rows", "cols"),
            P("rows", "cols"),
            P("cols", "rows"),
            P("rows", "cols"),
        ),
        out_specs=(P(None, ("cols", "rows")), P(None, "rows")),
        check_vma=False,
    )
```

profile of v0, /device:TPU:1, one launch (start us, length us, event | category | flops | bytes accessed | tf_op | source)
XLA Modules:
  0.0 1100.5 jit_solution(11856360554313025391)
XLA Ops:
  8.3 8.8 collective-permute-start.1
  17.1 1.9 collective-permute-start
  23.7 129.2 %psum.70 = f32[80]{0:T(128)S(1)} all-reduce(f32[80]{0:T(128)S(1)} %multiply_reduce_fusion.4), channel_id=1, replica_groups=mesh['rows'=64,'cols'=8] {'rows'}, use_global_device_ids=true, to_apply=%region_1.2 | all-reduce | flops 80 | bytes 640 | tf_op jit(solution)/shard_map/psum | solution.py:84
  153.7 3.0 fusion.30
  161.5 193.4 %all-reduce.6.cloned.1.call-done = f32[80,5120]{1,0:T(8,128)} async-done(((f32[80,5120]{1,0:T(8,128)}), f32[80,5120]{1,0:T(8,128)}) %all-reduce.6.cloned.1.call-update) | async-done | bytes 1638416 | tf_op jit(solution)/shard_map/psum | solution.py:87
  356.7 14.3 %psum.72 = f32[80]{0:T(128)S(1)} all-reduce(f32[80]{0:T(128)S(1)} %multiply_reduce_fusion.1), channel_id=1, replica_groups=mesh['rows'=64,'cols'=8] {'cols'}, use_global_device_ids=true, to_apply=%region_4.6 | all-reduce | flops 80 | bytes 640 | tf_op jit(solution)/shard_map/psum | solution.py:90
  372.2 2.2 gather_fusion.2
  374.4 4.4 fusion.8
  380.3 71.5 %all-reduce.8.cloned.1.call-done = bf16[80,512]{1,0:T(8,128)(2,1)} async-done(((bf16[80,512]{1,0:T(8,128)(2,1)}), bf16[80,512]{1,0:T(8,128)(2,1)}) %all-reduce.8.cloned.1.call-update) | async-done | bytes 81936 | tf_op jit(solution)/shard_map/psum | solution.py:75
  452.9 128.5 %psum.74 = f32[80]{0:T(128)S(1)} all-reduce(f32[80]{0:T(128)S(1)} %multiply_reduce_fusion.3), channel_id=1, replica_groups=mesh['rows'=64,'cols'=8] {'rows'}, use_global_device_ids=true, to_apply=%region_7.10 | all-reduce | flops 80 | bytes 640 | tf_op jit(solution)/shard_map/psum | solution.py:84
  584.3 3.0 fusion.28
  590.2 2.6 convolution_add_fusion
  592.9 188.6 %all-reduce.10.cloned.1.call-done = f32[80,5120]{1,0:T(8,128)} async-done(((f32[80,5120]{1,0:T(8,128)}), f32[80,5120]{1,0:T(8,128)}) %all-reduce.10.cloned.1.call-update) | async-done | bytes 1638416 | tf_op jit(solution)/shard_map/psum | solution.py:87
  781.4 2.5 multiply_reduce_fusion
  784.0 15.1 %psum.76 = f32[80]{0:T(128)} all-reduce(f32[80]{0:T(128)} %multiply_reduce_fusion), channel_id=1, replica_groups=mesh['rows'=64,'cols'=8] {'cols'}, use_global_device_ids=true, to_apply=%region_10.13 | all-reduce | flops 80 | bytes 640 | tf_op jit(solution)/shard_map/psum | solution.py:90
  802.5 3.4 gather_fusion.4
  806.0 4.4 fusion.6
  811.2 2.3 fusion.26
  813.6 71.5 %all-reduce.12.cloned.1.call-done = bf16[80,512]{1,0:T(8,128)(2,1)} async-done(((bf16[80,512]{1,0:T(8,128)(2,1)}), bf16[80,512]{1,0:T(8,128)(2,1)}) %all-reduce.12.cloned.1.call-update) | async-done | bytes 81936 | tf_op jit(solution)/shard_map/psum | solution.py:75
  886.8 128.9 %psum.78 = f32[80]{0:T(128)} all-reduce(f32[80]{0:T(128)} %multiply_reduce_fusion.2), channel_id=1, replica_groups=mesh['rows'=64,'cols'=8] {'rows'}, use_global_device_ids=true, to_apply=%region_13.16 | all-reduce | flops 80 | bytes 640 | tf_op jit(solution)/shard_map/psum | solution.py:84
  1017.2 2.5 fusion.88
  1020.6 2.3 gather_fusion.5
  1022.9 4.4 fusion.4
  1030.4 62.0 %all-reduce.14.cloned.1.call-done = bf16[80,512]{1,0:T(8,128)(2,1)} async-done(((bf16[80,512]{1,0:T(8,128)(2,1)}), bf16[80,512]{1,0:T(8,128)(2,1)}) %all-reduce.14.cloned.1.call-update) | async-done | bytes 81936 | tf_op jit(solution)/shard_map/psum | solution.py:75
  (107 shorter events, 34.9 us)
Async XLA Ops:
  7.2 152.4 %copy-start = (bf16[24,5120]{1,0:T(8,128)(2,1)S(1)}, bf16[24,5120]{1,0:T(8,128)(2,1)}, u32[]{:S(2)}) copy-start(bf16[24,5120]{1,0:T(8,128)(2,1)} %param.19) | copy-start | bytes 737284
  7.2 347.7 %all-reduce.6.cloned.1.call-start = ((), (), s32[]{:S(2)}) async-start(), calls=%async_computation | async-start | bytes 3276800 | tf_op jit(solution)/shard_map/psum | solution.py:87
  8.3 13.5 %collective-permute-start.1 = (f32[80,512]{0,1:T(8,128)S(1)}, f32[80,512]{0,1:T(8,128)S(1)}, u32[]{:S(2)}, u32[]{:S(2)}) collective-permute-start(f32[80,512]{0,1:T(8,128)S(1)} %copy.14), channel_id=1, source_target_pairs={{8,0},{16,8},{24,16},{32,24},{40,32},{48,40},{56,48},{64,56},{72,6... | collective-permute-start | bytes 491528 | tf_op jit(solution)/shard_map/ppermute | solution.py:21
  17.1 5.2 collective-permute-start
  21.8 565.5 %copy-start.11 = (bf16[30]{0:T(256)(128)(2,1)}, bf16[30]{0:T(256)(128)(2,1)S(1)}, u32[]{:S(2)}) copy-start(bf16[30]{0:T(256)(128)(2,1)S(1)} %compare_convert_fusion) | copy-start | bytes 184
  23.6 558.4 %copy-start.3 = (f32[512,80]{0,1:T(8,128)}, f32[512,80]{0,1:T(8,128)S(1)}, u32[]{:S(2)}) copy-start(f32[512,80]{0,1:T(8,128)S(1)} %copy.17) | copy-start | bytes 491524
  152.9 428.5 %copy-start.21 = (f32[80]{0:T(128)}, f32[80]{0:T(128)S(1)}, u32[]{:S(2)}) copy-start(f32[80]{0:T(128)S(1)} %psum.70) | copy-start | bytes 964
  161.4 290.4 %all-reduce.8.cloned.1.call-start = ((), (), s32[]{:S(2)}) async-start(), calls=%async_computation.1 | async-start | bytes 163840 | tf_op jit(solution)/shard_map/psum | solution.py:75
  161.5 210.7 %copy-start.15 = (s32[1024]{0:T(1024)}, s32[1024]{0:T(1024)S(1)}, u32[]{:S(2)}) copy-start(s32[1024]{0:T(1024)S(1)} %pad_clamp_fusion) | copy-start | bytes 12292
  161.5 212.9 %copy-start.23 = (pred[30]{0:T(512)(128)(4,1)}, pred[30]{0:T(512)(128)(4,1)S(1)}, u32[]{:S(2)}) copy-start(pred[30]{0:T(512)(128)(4,1)S(1)} %compare_and_fusion) | copy-start | bytes 94
  354.9 16.1 %copy-start.1 = (f32[80,5120]{1,0:T(8,128)S(1)}, f32[80,5120]{1,0:T(8,128)}, u32[]{:S(2)}) copy-start(f32[80,5120]{1,0:T(8,128)} %all-reduce.6.cloned.1.call-done) | copy-start | bytes 4915204
  374.4 4.4 copy-start.16
  374.4 4.6 copy-start.8
  380.2 401.2 %all-reduce.10.cloned.1.call-start = ((), (), s32[]{:S(2)}) async-start(), calls=%async_computation.2 | async-start | bytes 3276800 | tf_op jit(solution)/shard_map/psum | solution.py:87
  581.4 5.9 copy-start.22
  581.9 5.4 copy-start.14
  592.8 292.3 %all-reduce.12.cloned.1.call-start = ((), (), s32[]{:S(2)}) async-start(), calls=%async_computation.3 | async-start | bytes 163840 | tf_op jit(solution)/shard_map/psum | solution.py:75
  781.4 18.2 %copy-start.2 = (f32[80,5120]{1,0:T(8,128)S(1)}, f32[80,5120]{1,0:T(8,128)}, u32[]{:S(2)}) copy-start(f32[80,5120]{1,0:T(8,128)} %all-reduce.10.cloned.1.call-done) | copy-start | bytes 4915204
  806.0 4.4 copy-start.17
  813.6 278.8 %all-reduce.14.cloned.1.call-start = ((), (), s32[]{:S(2)}) async-start(), calls=%async_computation.4 | async-start | bytes 163840 | tf_op jit(solution)/shard_map/psum | solution.py:75
  1022.9 4.5 copy-start.13
  1022.9 4.5 copy-start.18
  1022.9 4.7 copy-start.6
  1022.9 69.4 %copy-start.4 = (f32[512,80]{0,1:T(8,128)S(1)}, f32[512,80]{0,1:T(8,128)}, u32[]{:S(2)}) copy-start(f32[512,80]{0,1:T(8,128)} %copy-done.3) | copy-start | bytes 491524
  (8 other events, 16.3 us)
Sparse Core Ops, SparseCore 0:
  161.5 193.3 all-reduce.5
  380.3 71.4 all-reduce.7
  592.9 188.4 all-reduce.9
  813.7 71.3 all-reduce.11
  1028.9 63.4 all-reduce.13
where the time goes:
time: 1100 us
  waiting for transfers between devices  588 us (53%)
  blocking collectives  416 us (38%)
  matrix products  33.1 us (3%)
  local copies, waits for them, and re-layouts  19.1 us (2%)
  other arithmetic  18.8 us (2%)
  between operations  14.9 us (1%)
    psum x3, blocking collectives, pixel_norm(): return jnp.sqrt(lax.psum(jnp.sum(field * field, axis=1), 'rows') + EPSILON)  387 us
    psum x2, waiting for transfers between devices, slip_update(): summed = lax.psum(partial_value, 'rows')  382 us
    psum x3, waiting for transfers between devices, apply_forward(): lax.psum((far_forward(vector_b, far_left, far_right) + near_term).astype(...  205 us
    psum x2, blocking collectives, slip_update(): squares = lax.psum(jnp.sum(summed * summed, axis=1), 'cols')  29.5 us
  transfers between devices with their start and end apart: 7, of which 6 were waited for; matrix products, arithmetic and copies ran while one was open for 0% of the time, Pallas kernels for 0%

commit v1 on v0

v1 whole, which is shorter than its diff:
```python
import functools

import jax
import jax.numpy as jnp
from jax import lax
from jax.experimental import pallas as pl
from jax.experimental.pallas import tpu as pltpu
from jax.sharding import PartitionSpec as P

EPSILON = 1e-06
LANE = 128
TILE = 16
MESH = pl.DeviceIdType.MESH
F32 = jnp.float32
BF16 = jnp.bfloat16

SCRATCH = (
    "tiles", "halo", "onehot", "g", "pc_send", "pc_recv", "px_send", "px_recv", "q_send", "q_recv", "v",
    "f_send", "f_recv", "f_all", "w1", "coef", "sa_send", "sa_recv", "sb_send", "sb_recv", "sz_send", "sz_recv",
    "tile_sem", "halo_ss", "halo_rs", "c_ss", "c_rs", "x_ss", "x_rs", "y_ss", "y_rs", "yg_ss", "yg_rs",
    "xg_ss", "xg_rs", "cg_ss", "cg_rs", "z_ss", "z_rs", "zg_ss", "zg_rs", "sa_ss", "sa_rs", "sb_ss", "sb_rs",
    "sz_ss", "sz_rs",
)


class Sizes:
    def __init__(self, dims, nz, realiz, pixels, width, slots, rank, tile_rows, tile_cols):
        self.nx, self.ny, self.cores = dims
        self.nz = nz
        self.rows = self.nx * self.ny * self.cores
        self.nq = self.nx * self.cores
        self.realiz, self.pixels, self.width = realiz, pixels, width
        self.slots, self.rank, self.tile_rows, self.tile_cols = slots, rank, tile_rows, tile_cols
        self.groups = realiz // TILE
        self.chunk = width // self.nq
        self.nb = self.chunk // LANE
        self.tb = self.nb * self.groups
        self.tp = -(-self.tb // self.ny)
        self.tq = self.tp * self.ny
        self.fb = pixels // LANE
        self.ft = self.fb * self.groups
        self.zp = -(-self.ft // nz)
        self.fz = self.zp * nz


def scratch_shapes(s):
    dma = pltpu.SemaphoreType.DMA
    return [
        pltpu.VMEM((s.slots, s.tile_rows, s.tile_cols), BF16),
        pltpu.VMEM((2, s.realiz, s.pixels), F32),
        pltpu.VMEM((3, s.pixels, s.pixels), BF16),
        pltpu.VMEM((s.nq, s.pixels, s.chunk), BF16),
        pltpu.VMEM((2, s.nx, s.tb, TILE, LANE), BF16),
        pltpu.VMEM((2, s.nx, s.tb, TILE, LANE), BF16),
        pltpu.VMEM((2, s.nx - 1, s.tb, TILE, LANE), BF16),
        pltpu.VMEM((2, s.nx - 1, s.tb, TILE, LANE), BF16),
        pltpu.VMEM((2, s.tq, TILE, LANE), BF16),
        pltpu.VMEM((2, s.ny - 1, s.tp, TILE, LANE), BF16),
        pltpu.VMEM((2, s.nq, s.tq, TILE, LANE), BF16),
        pltpu.VMEM((2, s.fz, TILE, LANE), BF16),
        pltpu.VMEM((2, s.nz - 1, s.zp, TILE, LANE), BF16),
        pltpu.VMEM((2, s.fz, TILE, LANE), BF16),
        pltpu.VMEM((s.tp, TILE, LANE), F32),
        pltpu.VMEM((2, s.groups, TILE, LANE), F32),
        pltpu.VMEM((3, 8, LANE), F32),
        pltpu.VMEM((3, s.nq - 1, 8, LANE), F32),
        pltpu.VMEM((3, 8, LANE), F32),
        pltpu.VMEM((3, s.ny - 1, 8, LANE), F32),
        pltpu.VMEM((2, 8, LANE), F32),
        pltpu.VMEM((2, s.nz - 1, 8, LANE), F32),
        dma((1,)),
        dma((1,)),
        dma((2,)),
        dma((2,)),
        dma((2, s.nx)),
        dma((2,)),
        dma((2, s.nx)),
        dma((2,)),
        dma((2,)),
        dma((2,)),
        dma((2,)),
        dma((2,)),
        dma((2, s.nx)),
        dma((2,)),
        dma((2, s.nx)),
        dma((2,)),
        dma((2,)),
        dma((2,)),
        dma((2,)),
        dma((3,)),
        dma((3,)),
        dma((3,)),
        dma((3,)),
        dma((2,)),
        dma((2,)),
    ]


def far_first(count):
    return sorted(range(1, count), key=lambda d: (-min(d, count - d), d))


def near_first(count):
    return sorted(range(1, count), key=lambda d: (min(d, count - d), d))


def await_bytes(ref, sem):
    pltpu.make_async_copy(ref, ref, sem).wait()


def to_row(column):
    rows = column.shape[0]
    wide = jnp.broadcast_to(column, (rows, LANE))
    wide = jnp.concatenate([wide, jnp.zeros((LANE - rows, LANE), F32)], axis=0)
    return wide.T[0:8]


def from_row(row, rows):
    return jnp.broadcast_to(row[0:1], (LANE, LANE)).T[0:rows]


def row_sums(blocks):
    total = blocks[0] * blocks[0]
    for block in blocks[1:]:
        total = total + block * block
    return jnp.sum(total, axis=1, keepdims=True)


def lane_blocks(value):
    return [value[:, j * LANE : (j + 1) * LANE] for j in range(value.shape[1] // LANE)]


def as_tiles(value):
    groups = value.shape[0] // TILE
    return jnp.concatenate([b.reshape(groups, TILE, LANE) for b in lane_blocks(value)], axis=0)


def from_tiles(tiles, groups):
    count = tiles.shape[0] // groups
    return jnp.concatenate(
        [tiles[j * groups : (j + 1) * groups].reshape(groups * TILE, LANE) for j in range(count)], axis=1
    )


def three_parts(value):
    high = value.astype(BF16)
    rest = value - high.astype(F32)
    middle = rest.astype(BF16)
    low = (rest - middle.astype(F32)).astype(BF16)
    return jnp.concatenate([high, middle, low], axis=0)


def kernel(s, data, source, slot_of, live, tiles_hbm, far_left, far_right, slip, misfit, *scratch):
    m = dict(zip(SCRATCH, scratch, strict=True))
    place = lax.axis_index("rows")
    z = lax.axis_index("cols")
    core = lax.rem(place, 2)
    chip = place // 2
    y = lax.rem(chip, s.ny)
    x = chip // s.ny
    other = 1 - core
    own_q = core * s.nx + x

    def at(xx, yy, cc):
        return ((xx * s.ny + yy) * 2 + cc, z)

    def cross(d):
        q = lax.rem(own_q + d, s.nq)
        return at(lax.rem(q, s.nx), y, q // s.nx)

    def along_y(d):
        return at(x, lax.rem(y + d, s.ny), core)

    def along_z(d):
        return (place, lax.rem(z + d, s.nz))

    mate = at(x, y, other)

    def send(src, dst, send_sem, recv_sem, device):
        pltpu.make_async_remote_copy(
            src_ref=src, dst_ref=dst, send_sem=send_sem, recv_sem=recv_sem, device_id=device, device_id_type=MESH
        ).start()

    tile_copy = pltpu.make_async_copy(tiles_hbm, m["tiles"], m["tile_sem"].at[0])
    tile_copy.start()

    step_out = lax.rem(place + s.rows + 2 * core - 1, s.rows)
    partners = [cross(d) for d in range(1, s.nq)]
    partners += [along_y(d) for d in range(1, s.ny)]
    partners += [along_z(d) for d in range(1, s.nz)]
    partners += [(step_out, z)]
    barrier = pltpu.get_barrier_semaphore()
    for device in partners:
        pl.semaphore_signal(barrier, inc=1, device_id=device, device_id_type=MESH)
    pl.semaphore_wait(barrier, len(partners))

    after = lax.rem(place + 1, s.rows)
    before = lax.rem(place + s.rows - 1, s.rows)
    send(data, m["halo"].at[0], m["halo_ss"].at[0], m["halo_rs"].at[0], (after, z))
    send(data, m["halo"].at[1], m["halo_ss"].at[0], m["halo_rs"].at[1], (before, z))

    total = s.rows * s.pixels
    offset = source[...] + s.pixels - place * s.pixels
    offset = jnp.where(offset < 0, offset + total, offset)
    offset = jnp.where(offset >= total, offset - total, offset)
    index = lax.broadcasted_iota(jnp.int32, (s.pixels, s.pixels), 0)
    for k in range(3):
        m["onehot"][k] = jnp.where(index == offset - k * s.pixels, 1.0, 0.0).astype(BF16)

    tile_copy.wait()
    per_row = s.width // s.tile_cols
    half = per_row // 2
    half_blocks = half * s.tile_cols // LANE
    bands = s.pixels // s.tile_rows

    def build(i, carry):
        g, a = i // bands, lax.rem(i, bands)
        pixel = pl.ds(pl.multiple_of(a * s.tile_rows, s.tile_rows), s.tile_rows)
        lefts = far_left[:, pixel]
        for b in range(half):
            where = a * per_row + g * half + b
            column = pl.ds(pl.multiple_of((g * half + b) * s.tile_cols, s.tile_cols), s.tile_cols)
            block = lax.dot_general(lefts, far_right[:, column], (((0,), (0,)), ((), ())), preferred_element_type=F32)
            block = block + m["tiles"][slot_of[where]].astype(F32) * live[where]
            block = block.astype(BF16)
            for k in range(s.tile_cols // LANE):
                j = b * (s.tile_cols // LANE) + k
                q = g * (half_blocks // s.nb) + j // s.nb
                lane = (j % s.nb) * LANE
                m["g"][q, pixel, lane : lane + LANE] = block[:, k * LANE : (k + 1) * LANE]
        return carry

    lax.fori_loop(0, 2 * bands, build, 0)

    seen = jnp.dot(three_parts(data[...]), m["onehot"][1], preferred_element_type=F32)
    for k in range(2):
        await_bytes(m["halo"].at[k], m["halo_rs"].at[k])
        seen = seen + jnp.dot(three_parts(m["halo"][k]), m["onehot"][2 * k], preferred_element_type=F32)
    n = s.realiz
    observed = (seen[0:n] + seen[n : 2 * n]) + seen[2 * n : 3 * n]
    misfit[...] = observed

    def sum_start(i, column):
        m["sa_send"][i] = to_row(column)
        for d in range(1, s.nq):
            send(m["sa_send"].at[i], m["sa_recv"].at[i, d - 1], m["sa_ss"].at[i], m["sa_rs"].at[i], cross(d))

    def sum_middle(i):
        await_bytes(m["sa_recv"].at[i], m["sa_rs"].at[i])
        m["sb_send"][i] = m["sa_send"][i] + jnp.sum(m["sa_recv"][i], axis=0)
        for d in range(1, s.ny):
            send(m["sb_send"].at[i], m["sb_recv"].at[i, d - 1], m["sb_ss"].at[i], m["sb_rs"].at[i], along_y(d))

    def sum_end(i):
        await_bytes(m["sb_recv"].at[i], m["sb_rs"].at[i])
        return from_row(m["sb_send"][i] + jnp.sum(m["sb_recv"][i], axis=0), n)

    def adjoint(it, pixel_b):
        def part(q):
            return as_tiles(jnp.dot(pixel_b, m["g"][q], preferred_element_type=F32))

        order = far_first(s.nx) + [0]
        for d in order:
            m["pc_send"][it, d] = part(other * s.nx + lax.rem(x + d, s.nx)).astype(BF16)
            send(m["pc_send"].at[it, d], m["pc_recv"].at[it, d], m["c_ss"].at[it], m["c_rs"].at[it, d], mate)
        own = None
        for d in order:
            xx = lax.rem(x + d, s.nx)
            own = part(core * s.nx + xx)
            await_bytes(m["pc_recv"].at[it, d], m["c_rs"].at[it, d])
            own = own + m["pc_recv"][it, d].astype(F32)
            if d > 0:
                m["px_send"][it, d - 1] = own.astype(BF16)
                send(
                    m["px_send"].at[it, d - 1],
                    m["px_recv"].at[it, d - 1],
                    m["x_ss"].at[it],
                    m["x_rs"].at[it, d - 1],
                    at(xx, y, core),
                )
        sum_middle(it)
        for d in near_first(s.nx):
            await_bytes(m["px_recv"].at[it, d - 1], m["x_rs"].at[it, d - 1])
            own = own + m["px_recv"][it, d - 1].astype(F32)
        m["q_send"][it, 0 : s.tb] = own.astype(BF16)
        if s.tq > s.tb:
            m["q_send"][it, s.tb : s.tq] = jnp.zeros((s.tq - s.tb, TILE, LANE), BF16)
        for d in far_first(s.ny):
            piece = pl.ds(lax.rem(y + d, s.ny) * s.tp, s.tp)
            send(
                m["q_send"].at[it, piece],
                m["q_recv"].at[it, d - 1],
                m["y_ss"].at[it],
                m["y_rs"].at[it],
                along_y(d),
            )
        await_bytes(m["q_recv"].at[it], m["y_rs"].at[it])
        share = m["q_send"][it, pl.ds(y * s.tp, s.tp)].astype(F32)
        for d in range(s.ny - 1):
            share = share + m["q_recv"][it, d].astype(F32)
        return share

    def forward(it, share):
        v = m["v"]
        mine = v.at[it, own_q, pl.ds(y * s.tp, s.tp)]
        mine[...] = share.astype(BF16)
        for d in far_first(s.ny):
            send(mine, mine, m["yg_ss"].at[it], m["yg_rs"].at[it], along_y(d))
        await_bytes(m["q_recv"].at[it], m["yg_rs"].at[it])
        ready = v.at[it, own_q, 0 : s.tb]
        for d in far_first(s.nx):
            send(ready, ready, m["xg_ss"].at[it], m["xg_rs"].at[it, d - 1], at(lax.rem(x + d, s.nx), y, core))
        send(ready, ready, m["cg_ss"].at[it], m["cg_rs"].at[it, 0], mate)

        def part(q):
            return lax.dot_general(
                from_tiles(v[it, q, 0 : s.tb], s.groups),
                m["g"][q],
                (((1,), (1,)), ((), ())),
                preferred_element_type=F32,
            )

        total = part(own_q)
        for d in near_first(s.nx):
            q = core * s.nx + lax.rem(x + s.nx - d, s.nx)
            came = v.at[it, q, 0 : s.tb]
            await_bytes(came, m["xg_rs"].at[it, d - 1])
            send(came, came, m["cg_ss"].at[it], m["cg_rs"].at[it, d], mate)
            total = total + part(q)
        for d in [0] + near_first(s.nx):
            q = other * s.nx + lax.rem(x + s.nx - d, s.nx)
            await_bytes(v.at[it, q, 0 : s.tb], m["cg_rs"].at[it, d])
            total = total + part(q)

        m["f_send"][it, 0 : s.ft] = as_tiles(total).astype(BF16)
        if s.fz > s.ft:
            m["f_send"][it, s.ft : s.fz] = jnp.zeros((s.fz - s.ft, TILE, LANE), BF16)
        for d in far_first(s.nz):
            piece = pl.ds(lax.rem(z + d, s.nz) * s.zp, s.zp)
            send(
                m["f_send"].at[it, piece],
                m["f_recv"].at[it, d - 1],
                m["z_ss"].at[it],
                m["z_rs"].at[it],
                along_z(d),
            )

        def squares(q, running):
            for j in range(s.nb):
                block = v[it, q, j * s.groups : (j + 1) * s.groups].astype(F32).reshape(n, LANE)
                running = running + block * block
            return running

        running = lax.fori_loop(0, s.nq, squares, jnp.zeros((n, LANE), F32))
        m["sz_send"][it] = to_row(jnp.sum(running, axis=1, keepdims=True))
        for d in far_first(s.nz):
            send(m["sz_send"].at[it], m["sz_recv"].at[it, d - 1], m["sz_ss"].at[it], m["sz_rs"].at[it], along_z(d))

        await_bytes(m["f_recv"].at[it], m["z_rs"].at[it])
        reduced = m["f_send"][it, pl.ds(z * s.zp, s.zp)].astype(F32)
        for d in range(s.nz - 1):
            reduced = reduced + m["f_recv"][it, d].astype(F32)
        mine = m["f_all"].at[it, pl.ds(z * s.zp, s.zp)]
        mine[...] = reduced.astype(BF16)
        for d in far_first(s.nz):
            send(mine, mine, m["zg_ss"].at[it], m["zg_rs"].at[it], along_z(d))
        await_bytes(m["sz_recv"].at[it], m["sz_rs"].at[it])
        norm2 = from_row(m["sz_send"][it] + jnp.sum(m["sz_recv"][it], axis=0), n)
        return norm2

    def predicted(it):
        return [
            m["f_all"][it, j * s.groups : (j + 1) * s.groups].astype(F32).reshape(n, LANE) for j in range(s.fb)
        ]

    def gathered(it):
        await_bytes(m["f_recv"].at[it], m["zg_rs"].at[it])
        return predicted(it)

    sum_start(0, row_sums(lane_blocks(observed)))
    w1 = adjoint(0, observed.astype(BF16))
    m["w1"][...] = w1
    norm2 = forward(0, w1)
    beta1 = jnp.sqrt(sum_end(0) + EPSILON)
    alpha1 = jnp.sqrt(norm2 / (beta1 * beta1) + EPSILON)
    scale1 = 1.0 / (beta1 * alpha1)
    ratio = alpha1 / beta1
    seen = lane_blocks(misfit[...])
    left = [f * scale1 - ratio * o for f, o in zip(gathered(0), seen, strict=True)]

    sum_start(1, row_sums(left))
    w2 = adjoint(1, jnp.concatenate(left, axis=1).astype(BF16))
    beta2 = jnp.sqrt(sum_end(1) + EPSILON)
    m["coef"][0] = (1.0 / beta2).reshape(s.groups, TILE, LANE)
    m["coef"][1] = (beta2 * scale1).reshape(s.groups, TILE, LANE)
    share = []
    for i in range(s.tp):
        group = lax.rem(y * s.tp + i, s.groups)
        share.append(w2[i] * m["coef"][0, group] - m["w1"][i] * m["coef"][1, group])
    norm2 = forward(1, jnp.stack(share, axis=0))
    alpha2 = jnp.sqrt(norm2 + EPSILON)
    inverse2 = 1.0 / alpha2
    ratio = alpha2 / beta2
    left = [f * inverse2 - ratio * o for f, o in zip(gathered(1), left, strict=True)]

    sum_start(2, row_sums(left))
    rho1 = jnp.sqrt(alpha1 * alpha1 + beta2 * beta2)
    cosine, sine = alpha1 / rho1, beta2 / rho1
    phi1 = cosine * beta1
    phibar = sine * beta1
    theta = sine * alpha2
    rhobar = -cosine * alpha2

    first = place * (s.width // s.rows)
    block = first // LANE
    lane = lax.rem(first, LANE)
    share_width = s.width // s.rows
    cover = -(-share_width // LANE)
    shape = ((cover + 1) * LANE, cover * LANE)
    pick = lax.broadcasted_iota(jnp.int32, shape, 0) == lax.broadcasted_iota(jnp.int32, shape, 1) + lane
    pick = jnp.where(pick, 1.0, 0.0).astype(BF16)
    window = []
    for it in range(2):
        sides = []
        for k in range(cover + 1):
            b = jnp.minimum(block + k, s.width // LANE - 1)
            sides.append(m["v"][it, b // s.nb, pl.ds(lax.rem(b, s.nb) * s.groups, s.groups)].reshape(n, LANE))
        window.append(jnp.dot(jnp.concatenate(sides, axis=1), pick, preferred_element_type=F32))

    sum_middle(2)
    beta3 = jnp.sqrt(sum_end(2) + EPSILON)
    rho2 = jnp.sqrt(rhobar * rhobar + beta3 * beta3)
    phi2 = rhobar / rho2 * phibar
    on2 = phi2 / rho2
    weight1 = (phi1 / rho1 - on2 * (theta / rho1)) * scale1
    weight2 = on2 * inverse2
    result = [weight1 * a + weight2 * b for a, b in zip(lane_blocks(window[0]), lane_blocks(window[1]), strict=True)]
    slip[...] = jnp.concatenate(result, axis=1)[:, 0:share_width]
    for j, (f1, f2, o) in enumerate(zip(predicted(0), predicted(1), seen, strict=True)):
        misfit[:, j * LANE : (j + 1) * LANE] = o - weight1 * f1 - weight2 * f2

    await_bytes(m["halo"], m["halo_ss"].at[0])
    for it in range(2):
        await_bytes(m["pc_send"].at[it], m["c_ss"].at[it])
        await_bytes(m["px_send"].at[it], m["x_ss"].at[it])
        await_bytes(m["q_recv"].at[it], m["y_ss"].at[it])
        await_bytes(m["q_recv"].at[it], m["yg_ss"].at[it])
        await_bytes(m["px_send"].at[it], m["xg_ss"].at[it])
        await_bytes(m["pc_send"].at[it], m["cg_ss"].at[it])
        await_bytes(m["f_recv"].at[it], m["z_ss"].at[it])
        await_bytes(m["f_recv"].at[it], m["zg_ss"].at[it])
        await_bytes(m["sz_recv"].at[it], m["sz_ss"].at[it])
    for i in range(3):
        await_bytes(m["sa_recv"].at[i], m["sa_ss"].at[i])
        await_bytes(m["sb_recv"].at[i], m["sb_ss"].at[i])


def body(dims, nz, data, source, near_tiles, near_rows, near_cols, near_count, far_left, far_right):
    realiz, pixels = data.shape
    rank, width = far_right.shape
    slots, tile_rows, tile_cols = near_tiles.shape
    s = Sizes(dims, nz, realiz, pixels, width, slots, rank, tile_rows, tile_cols)
    per_row = width // tile_cols
    positions = pixels // tile_rows * per_row
    slot = jnp.arange(slots, dtype=jnp.int32)
    where = jnp.where(slot < near_count[0, 0], near_rows[:, 0] * per_row + near_cols[:, 0], -1)
    found = where[None, :] == jnp.arange(positions, dtype=jnp.int32)[:, None]
    slot_of = jnp.sum(jnp.where(found, slot[None, :], 0), axis=1)
    live = jnp.sum(jnp.where(found, 1.0, 0.0), axis=1)
    vmem = pl.BlockSpec(memory_space=pltpu.VMEM)
    smem = pl.BlockSpec(memory_space=pltpu.SMEM)
    return pl.pallas_call(
        functools.partial(kernel, s),
        out_shape=(
            jax.ShapeDtypeStruct((realiz, width // s.rows), F32),
            jax.ShapeDtypeStruct((realiz, pixels), F32),
        ),
        in_specs=[vmem, vmem, smem, smem, pl.BlockSpec(memory_space=pl.ANY), vmem, vmem],
        out_specs=(vmem, vmem),
        scratch_shapes=scratch_shapes(s),
        compiler_params=pltpu.CompilerParams(
            collective_id=0, has_side_effects=True, vmem_limit_bytes=48 * 1024 * 1024
        ),
    )(data, source.reshape(1, pixels), slot_of, live, near_tiles, far_left, far_right)


def solution(mesh, dims=(4, 8, 2)):
    return jax.shard_map(
        functools.partial(body, dims, mesh.shape["cols"]),
        mesh=mesh,
        in_specs=(
            P(None, "rows"),
            P("rows"),
            P("rows", "cols", None),
            P("rows", "cols"),
            P("rows", "cols"),
            P("rows", "cols"),
            P("cols", "rows"),
            P("rows", "cols"),
        ),
        out_specs=(P(None, ("cols", "rows")), P(None, "rows")),
        check_vma=False,
    )
```

time: 1100 us -> 111 us (0.10)
  waiting for transfers between devices: 588 us -> 0 us
  blocking collectives: 416 us -> 0 us
  Pallas kernels: 0 us -> 102 us
  matrix products: 33.1 us -> 0 us
  other arithmetic: 18.8 us -> 0.86 us
  between operations: 14.9 us -> 1.29 us
  local copies, waits for them, and re-layouts: 19.1 us -> 6.67 us
    psum x5 -> x0, waiting for transfers between devices: 587 us -> none  [the longest x2 382 us: slip_update(): summed = lax.psum(partial_value, 'rows')]
    psum x5 -> x0, blocking collectives: 416 us -> none  [the longest x3 387 us: pixel_norm(): return jnp.sqrt(lax.psum(jnp.sum(field * field, axis=1), 'rows') + EPSILON)]
    pallas_call x0 -> x1, Pallas kernels: none -> 102 us  [body(): pl.pallas_call(functools.partial(kernel, s), out_shape=(jax.ShapeDtypeStr...]
    dot_general x15 -> x0, matrix products: 33.1 us -> none  [the longest x3 13.2 us: padded_forward(): jnp.einsum('knq,npq->nkp', pieces, tiles, preferred_element_type=jnp.floa...]
  transfers between devices with their start and end apart: 7 -> 0, of which waited for: 6 -> 0; matrix products, arithmetic and copies ran while one was open for 0% -> 0% of each run, Pallas kernels for 0% -> 0%
where the time goes in v1:
time: 111 us
  Pallas kernels  102 us (92%)
  local copies, waits for them, and re-layouts  6.67 us (6%)
  between operations  1.29 us (1%)
    pallas_call x1, Pallas kernels, body(): pl.pallas_call(functools.partial(kernel, s), out_shape=(jax.ShapeDtypeStr...  102 us
    unnamed x12, local copies, waits for them, and re-layouts  6.67 us

profile of v1, /device:TPU:1, one launch (start us, length us, event | category | flops | bytes accessed | tf_op | source)
XLA Modules:
  0.0 110.7 jit_solution(3990693150085521193)
XLA Ops:
  1.3 0.7 compare_select_fusion
  2.0 0.1 select_reduce_fusion.live
  2.0 0.1 select_reduce_fusion.1.slot_of
  2.1 0.0 copy-start
  2.1 2.1 %copy-done = bf16[30,128,512]{2,1,0:T(8,128)(2,1)S(1)} copy-done((bf16[30,128,512]{2,1,0:T(8,128)(2,1)S(1)}, bf16[30,128,512]{2,1,0:T(8,128)(2,1)}, u32[]{:S(2)}) %copy-start) | copy-done | bytes 3932184
  4.3 0.0 copy-start.1
  4.3 0.9 copy-done.1
  5.2 0.0 copy-start.2
  5.2 0.9 copy-done.2
  6.1 0.0 copy-start.3
  6.1 0.7 copy-done.3
  6.8 0.0 copy-start.4
  6.9 0.7 copy-done.4
  7.5 101.9 %shard_map.95 = (f32[80,80]{1,0:T(8,128)S(1)}, f32[80,512]{1,0:T(8,128)S(1)}) custom-call(f32[80,512]{1,0:T(8,128)S(1)} %copy-done.2, s32[1,512]{1,0:T(1,128)S(1)} %bitcast.5, s32[40]{0:T(128)S(1)} %select_reduce_fusion.1.slot_of, f32[40]{0:T(128)S(1)} %select_reduce_fusion.live, bf16[30,128,512]{2,1,0:T(8,128)(2,1)S(1)} %copy-done, ...), custom_call_target="tpu_custom_call" | custom-call | tf_op jit(solution)/shard_map/pallas_call | solution.py:472
  109.4 0.6 copy.13
  110.0 0.7 copy.14
Async XLA Ops:
  2.1 2.1 %copy-start = (bf16[30,128,512]{2,1,0:T(8,128)(2,1)S(1)}, bf16[30,128,512]{2,1,0:T(8,128)(2,1)}, u32[]{:S(2)}) copy-start(bf16[30,128,512]{2,1,0:T(8,128)(2,1)} %tiles_hbm.1) | copy-start | bytes 11796484
  4.3 0.9 copy-start.1
  5.2 0.9 copy-start.2
  6.1 0.7 copy-start.3
  6.8 0.7 copy-start.4

commit v2 on v1

v2 whole, which is shorter than its diff:
```python
import functools

import jax
import jax.numpy as jnp
from jax import lax
from jax.experimental import pallas as pl
from jax.experimental.pallas import tpu as pltpu
from jax.sharding import PartitionSpec as P

EPSILON = 1e-06
LANE = 128
TILE = 16
MESH = pl.DeviceIdType.MESH
F32 = jnp.float32
BF16 = jnp.bfloat16


class Part:
    def __init__(self, first, blocks, groups, ny):
        self.lanes = slice(first * LANE, (first + blocks) * LANE)
        self.blocks = blocks
        self.tb = blocks * groups
        self.tp = -(-self.tb // ny)
        self.tq = self.tp * ny
        self.half = (self.tb + 1) // 2


class Sizes:
    def __init__(self, dims, nz, realiz, pixels, width, slots, rank, tile_rows, tile_cols):
        self.nx, self.ny, self.cores = dims
        self.nz = nz
        self.rows = self.nx * self.ny * self.cores
        self.nq = self.nx * self.cores
        self.realiz, self.pixels, self.width = realiz, pixels, width
        self.slots, self.rank, self.tile_rows, self.tile_cols = slots, rank, tile_rows, tile_cols
        self.groups = realiz // TILE
        self.chunk = width // self.nq
        self.nb = self.chunk // LANE
        self.cut = (self.nb + 1) // 2
        self.parts = [
            Part(0, self.cut, self.groups, self.ny),
            Part(self.cut, self.nb - self.cut, self.groups, self.ny),
        ]
        self.tb = max(p.tb for p in self.parts)
        self.tp = max(p.tp for p in self.parts)
        self.tq = max(p.tq for p in self.parts)
        self.fb = pixels // LANE
        self.ft = self.fb * self.groups
        self.zp = -(-self.ft // nz)
        self.fz = self.zp * nz


def scratch_shapes(s):
    dma = pltpu.SemaphoreType.DMA
    tile = (TILE, LANE)
    return [
        pltpu.VMEM((s.realiz, s.pixels), F32),
        pltpu.VMEM((1, s.pixels), jnp.int32),
        pltpu.VMEM((s.slots, s.tile_rows, s.tile_cols), BF16),
        pltpu.VMEM((s.rank, s.pixels), BF16),
        pltpu.VMEM((s.rank, s.width), BF16),
        pltpu.SMEM((s.slots,), jnp.int32),
        pltpu.SMEM((s.slots,), jnp.int32),
        pltpu.SMEM((1, 1), jnp.int32),
        pltpu.VMEM((8, LANE), jnp.int32),
        pltpu.SMEM((8, LANE), jnp.int32),
        pltpu.VMEM((2, s.realiz, s.pixels), F32),
        pltpu.VMEM((3, s.pixels, s.pixels), BF16),
        pltpu.VMEM((s.nq, s.pixels, s.chunk), BF16),
        pltpu.VMEM((2, 2, s.nx, s.tb, *tile), BF16),
        pltpu.VMEM((2, 2, s.nx, s.tb, *tile), BF16),
        pltpu.VMEM((2, 2, 3, s.tb, *tile), BF16),
        pltpu.VMEM((2, 2, 3, s.tb, *tile), BF16),
        pltpu.VMEM((2, 2, s.tq, *tile), BF16),
        pltpu.VMEM((2, 2, s.ny - 1, s.tp, *tile), BF16),
        pltpu.VMEM((2, s.nq, 2, s.tq, *tile), BF16),
        pltpu.VMEM((2, s.fz, *tile), BF16),
        pltpu.VMEM((2, s.nz - 1, s.zp, *tile), BF16),
        pltpu.VMEM((2, s.fz, *tile), BF16),
        pltpu.VMEM((2, s.tp, *tile), F32),
        pltpu.VMEM((2, s.groups, *tile), F32),
        pltpu.VMEM((3, 8, LANE), F32),
        pltpu.VMEM((3, s.nq - 1, 8, LANE), F32),
        pltpu.VMEM((3, 8, LANE), F32),
        pltpu.VMEM((3, s.ny - 1, 8, LANE), F32),
        pltpu.VMEM((2, 8, LANE), F32),
        pltpu.VMEM((2, s.nz - 1, 8, LANE), F32),
        dma((9,)),
        dma((1,)),
        dma((2,)),
        dma((2, 2)),
        dma((2, 2, s.nx)),
        dma((2, 2)),
        dma((2, 2, 4)),
        dma((2, 2)),
        dma((2, 2)),
        dma((2, 2)),
        dma((2, 2)),
        dma((2, 2)),
        dma((2, 2, 4)),
        dma((2, 2)),
        dma((2, 2, 5)),
        dma((2,)),
        dma((2,)),
        dma((2,)),
        dma((2,)),
        dma((3,)),
        dma((3,)),
        dma((3,)),
        dma((3,)),
        dma((2,)),
        dma((2,)),
    ]


def far_first(count):
    return sorted(range(1, count), key=lambda d: (-min(d, count - d), d))


def near_first(count):
    return sorted(range(1, count), key=lambda d: (min(d, count - d), d))


def await_bytes(ref, sem):
    pltpu.make_async_copy(ref, ref, sem).wait()


def to_row(column):
    rows = column.shape[0]
    wide = jnp.broadcast_to(column, (rows, LANE))
    wide = jnp.concatenate([wide, jnp.zeros((LANE - rows, LANE), F32)], axis=0)
    return wide.T[0:8]


def from_row(row, rows):
    return jnp.broadcast_to(row[0:1], (LANE, LANE)).T[0:rows]


def row_sums(blocks):
    total = blocks[0] * blocks[0]
    for block in blocks[1:]:
        total = total + block * block
    return jnp.sum(total, axis=1, keepdims=True)


def lane_blocks(value):
    return [value[:, j * LANE : (j + 1) * LANE] for j in range(value.shape[1] // LANE)]


def as_tiles(value):
    groups = value.shape[0] // TILE
    return jnp.concatenate([b.reshape(groups, TILE, LANE) for b in lane_blocks(value)], axis=0)


def from_tiles(tiles, groups):
    count = tiles.shape[0] // groups
    return jnp.concatenate(
        [tiles[j * groups : (j + 1) * groups].reshape(groups * TILE, LANE) for j in range(count)], axis=1
    )


def three_parts(value):
    high = value.astype(BF16)
    rest = value - high.astype(F32)
    middle = rest.astype(BF16)
    low = (rest - middle.astype(F32)).astype(BF16)
    return jnp.concatenate([high, middle, low], axis=0)


def kernel(
    s, data_hbm, source_hbm, rows_hbm, cols_hbm, count_hbm, tiles_hbm, left_hbm, right_hbm, slip, misfit,
    data, source, tiles, far_left, far_right, near_rows, near_cols, near_count, table, table_s, halo, onehot, g,
    pc_send, pc_recv, px_send, px_recv, q_send, q_recv, v, f_send, f_recv, f_all, w1, coef, sa_send, sa_recv,
    sb_send, sb_recv, sz_send, sz_recv, in_sem, halo_ss, halo_rs, c_ss, c_rs, x_ss, x_rs, y_ss, y_rs, yg_ss,
    yg_rs, xg_ss, xg_rs, cg_ss, cg_rs, z_ss, z_rs, zg_ss, zg_rs, sa_ss, sa_rs, sb_ss, sb_rs, sz_ss, sz_rs,
):
    place = lax.axis_index("rows")
    z = lax.axis_index("cols")
    core = lax.rem(place, 2)
    chip = place // 2
    y = lax.rem(chip, s.ny)
    x = chip // s.ny
    other = 1 - core
    own_q = core * s.nx + x
    n = s.realiz

    def at(xx, yy, cc):
        return ((xx * s.ny + yy) * 2 + cc, z)

    def cross(d):
        q = lax.rem(own_q + d, s.nq)
        return at(lax.rem(q, s.nx), y, q // s.nx)

    def along_y(d):
        return at(x, lax.rem(y + d, s.ny), core)

    def along_z(d):
        return (place, lax.rem(z + d, s.nz))

    def beside(d):
        return lax.rem(x + d + s.nx, s.nx)

    mate = at(x, y, other)
    up = at(beside(1), y, core)
    down = at(beside(-1), y, core)

    def send(src, dst, send_sem, recv_sem, device):
        pltpu.make_async_remote_copy(
            src_ref=src, dst_ref=dst, send_sem=send_sem, recv_sem=recv_sem, device_id=device, device_id_type=MESH
        ).start()

    pairs = [
        (rows_hbm, near_rows),
        (cols_hbm, near_cols),
        (count_hbm, near_count),
        (source_hbm, source),
        (data_hbm, data),
        (left_hbm, far_left),
        (right_hbm, far_right),
        (tiles_hbm, tiles),
    ]
    loads = [pltpu.make_async_copy(src, dst, in_sem.at[k]) for k, (src, dst) in enumerate(pairs)]
    for load in loads:
        load.start()

    step_out = lax.rem(place + s.rows + 2 * core - 1, s.rows)
    partners = [cross(d) for d in range(1, s.nq)]
    partners += [along_y(d) for d in range(1, s.ny)]
    partners += [along_z(d) for d in range(1, s.nz)]
    partners += [(step_out, z)]
    barrier = pltpu.get_barrier_semaphore()
    for device in partners:
        pl.semaphore_signal(barrier, inc=1, device_id=device, device_id_type=MESH)

    for load in loads[:3]:
        load.wait()
    per_row = s.width // s.tile_cols
    spot = lax.broadcasted_iota(jnp.int32, (8, LANE), 1)
    slot_of = jnp.full((8, LANE), -1, jnp.int32)
    for k in range(s.slots):
        where = jnp.where(k < near_count[0, 0], near_rows[k] * per_row + near_cols[k], -1)
        slot_of = jnp.where(spot == where, k, slot_of)
    table[...] = slot_of
    to_scalars = pltpu.make_async_copy(table, table_s, in_sem.at[8])
    to_scalars.start()

    pl.semaphore_wait(barrier, len(partners))

    after = lax.rem(place + 1, s.rows)
    before = lax.rem(place + s.rows - 1, s.rows)
    loads[4].wait()
    send(data, halo.at[0], halo_ss.at[0], halo_rs.at[0], (after, z))
    send(data, halo.at[1], halo_ss.at[0], halo_rs.at[1], (before, z))

    loads[3].wait()
    total = s.rows * s.pixels
    offset = source[...] + s.pixels - place * s.pixels
    offset = jnp.where(offset < 0, offset + total, offset)
    offset = jnp.where(offset >= total, offset - total, offset)
    index = lax.broadcasted_iota(jnp.int32, (s.pixels, s.pixels), 0)
    for k in range(3):
        onehot[k] = jnp.where(index == offset - k * s.pixels, 1.0, 0.0).astype(BF16)

    for load in loads[5:]:
        load.wait()
    to_scalars.wait()
    half = per_row // 2
    half_blocks = half * s.tile_cols // LANE
    bands = s.pixels // s.tile_rows

    def build(i, carry):
        side, a = i // bands, lax.rem(i, bands)
        pixel = pl.ds(pl.multiple_of(a * s.tile_rows, s.tile_rows), s.tile_rows)
        lefts = far_left[:, pixel]
        for b in range(half):
            column = pl.ds(pl.multiple_of((side * half + b) * s.tile_cols, s.tile_cols), s.tile_cols)
            block = lax.dot_general(lefts, far_right[:, column], (((0,), (0,)), ((), ())), preferred_element_type=F32)
            slot = table_s[0, a * per_row + side * half + b]
            near = tiles[jnp.maximum(slot, 0)].astype(F32)
            block = (block + near * jnp.where(slot >= 0, 1.0, 0.0)).astype(BF16)
            for k in range(s.tile_cols // LANE):
                j = b * (s.tile_cols // LANE) + k
                q = side * (half_blocks // s.nb) + j // s.nb
                lane = (j % s.nb) * LANE
                g[q, pixel, lane : lane + LANE] = block[:, k * LANE : (k + 1) * LANE]
        return carry

    lax.fori_loop(0, 2 * bands, build, 0)

    seen = jnp.dot(three_parts(data[...]), onehot[1], preferred_element_type=F32)
    for k in range(2):
        await_bytes(halo.at[k], halo_rs.at[k])
        seen = seen + jnp.dot(three_parts(halo[k]), onehot[2 * k], preferred_element_type=F32)
    observed = (seen[0:n] + seen[n : 2 * n]) + seen[2 * n : 3 * n]
    misfit[...] = observed

    def sum_start(i, column):
        sa_send[i] = to_row(column)
        for d in range(1, s.nq):
            send(sa_send.at[i], sa_recv.at[i, d - 1], sa_ss.at[i], sa_rs.at[i], cross(d))

    def sum_middle(i):
        await_bytes(sa_recv.at[i], sa_rs.at[i])
        sb_send[i] = sa_send[i] + jnp.sum(sa_recv[i], axis=0)
        for d in range(1, s.ny):
            send(sb_send.at[i], sb_recv.at[i, d - 1], sb_ss.at[i], sb_rs.at[i], along_y(d))

    def sum_end(i):
        await_bytes(sb_recv.at[i], sb_rs.at[i])
        return from_row(sb_send[i] + jnp.sum(sb_recv[i], axis=0), n)

    def adjoint(it, pixel_b, column):
        def product(q, p):
            return as_tiles(jnp.dot(pixel_b, g[q, :, s.parts[p].lanes], preferred_element_type=F32))

        def to_mate(d, p):
            tb = s.parts[p].tb
            mine = pc_send.at[it, p, d, 0:tb]
            mine[...] = product(other * s.nx + beside(d), p).astype(BF16)
            send(mine, pc_recv.at[it, p, d, 0:tb], c_ss.at[it, p], c_rs.at[it, p, d], mate)

        def pair_sum(d, p):
            own = product(core * s.nx + beside(d), p)
            came = pc_recv.at[it, p, d, 0 : s.parts[p].tb]
            await_bytes(came, c_rs.at[it, p, d])
            return own + came[...].astype(F32)

        def relay_out(p):
            tb, cut = s.parts[p].tb, s.parts[p].half
            px_send[it, p, 0, 0:tb] = pair_sum(2, p).astype(BF16)
            for k, (lo, hi, device) in enumerate(((0, cut, up), (cut, tb, down))):
                send(
                    px_send.at[it, p, 0, lo:hi],
                    px_recv.at[it, p, 2, lo:hi],
                    x_ss.at[it, p],
                    x_rs.at[it, p, 2 + k],
                    device,
                )

        def relay_on(k, p):
            tb, cut = s.parts[p].tb, s.parts[p].half
            lo, hi = ((0, cut), (cut, tb))[k]
            own = pair_sum((1, 3)[k], p)
            came = px_recv.at[it, p, 2, lo:hi]
            await_bytes(came, x_rs.at[it, p, 2 + k])
            passed = own[lo:hi] + came[...].astype(F32)
            own = jnp.concatenate([passed, own[hi:]] if k == 0 else [own[:lo], passed], axis=0)
            px_send[it, p, 1 + k, 0:tb] = own.astype(BF16)
            send(
                px_send.at[it, p, 1 + k, 0:tb],
                px_recv.at[it, p, k, 0:tb],
                x_ss.at[it, p],
                x_rs.at[it, p, k],
                (up, down)[k],
            )

        def scatter_y(p):
            tb, tp, tq = s.parts[p].tb, s.parts[p].tp, s.parts[p].tq
            own = pair_sum(0, p)
            for k in range(2):
                came = px_recv.at[it, p, k, 0:tb]
                await_bytes(came, x_rs.at[it, p, k])
                own = own + came[...].astype(F32)
            q_send[it, p, 0:tb] = own.astype(BF16)
            if tq > tb:
                q_send[it, p, tb:tq] = jnp.zeros((tq - tb, TILE, LANE), BF16)
            for d in far_first(s.ny):
                piece = pl.ds(lax.rem(y + d, s.ny) * tp, tp)
                send(
                    q_send.at[it, p, piece],
                    q_recv.at[it, p, d - 1, 0:tp],
                    y_ss.at[it, p],
                    y_rs.at[it, p],
                    along_y(d),
                )

        to_mate(2, 0)
        to_mate(2, 1)
        to_mate(1, 0)
        to_mate(3, 0)
        relay_out(0)
        relay_out(1)
        sum_start(it, column)
        to_mate(1, 1)
        to_mate(3, 1)
        relay_on(0, 0)
        relay_on(1, 0)
        to_mate(0, 0)
        to_mate(0, 1)
        relay_on(0, 1)
        relay_on(1, 1)
        sum_middle(it)
        scatter_y(0)
        scatter_y(1)

    def y_share(it, p):
        tp = s.parts[p].tp
        await_bytes(q_recv.at[it, p, :, 0:tp], y_rs.at[it, p])
        share = q_send[it, p, pl.ds(y * tp, tp)].astype(F32)
        for d in range(s.ny - 1):
            share = share + q_recv[it, p, d, 0:tp].astype(F32)
        return share

    def spread_y(it, p, share):
        tp = s.parts[p].tp
        mine = v.at[it, own_q, p, pl.ds(y * tp, tp)]
        mine[...] = share.astype(BF16)
        for d in far_first(s.ny):
            send(mine, mine, yg_ss.at[it, p], yg_rs.at[it, p], along_y(d))

    def forward(it):
        def product(q, p):
            return lax.dot_general(
                from_tiles(v[it, q, p, 0 : s.parts[p].tb], s.groups),
                g[q, :, s.parts[p].lanes],
                (((1,), (1,)), ((), ())),
                preferred_element_type=F32,
            )

        def pass_x(q, p, lo, hi, k, device):
            piece = v.at[it, q, p, lo:hi]
            send(piece, piece, xg_ss.at[it, p], xg_rs.at[it, p, k], device)

        def pass_mate(q, p, lo, hi, k):
            piece = v.at[it, q, p, lo:hi]
            send(piece, piece, cg_ss.at[it, p], cg_rs.at[it, p, k], mate)

        total = jnp.zeros((n, s.pixels), F32)
        for p, part in enumerate(s.parts):
            await_bytes(q_recv.at[it, p, :, 0 : part.tp], yg_rs.at[it, p])
            pass_x(own_q, p, 0, part.tb, 0, up)
            pass_x(own_q, p, 0, part.tb, 1, down)
            pass_mate(own_q, p, 0, part.tb, 0)
            total = total + product(own_q, p)
        for p, part in enumerate(s.parts):
            for k in range(2):
                q = core * s.nx + beside((-1, 1)[k])
                lo, hi = ((0, part.half), (part.half, part.tb))[k]
                await_bytes(v.at[it, q, p, 0 : part.tb], xg_rs.at[it, p, k])
                pass_x(q, p, lo, hi, 2 + k, (up, down)[k])
                pass_mate(q, p, 0, part.tb, 1 + k)
                total = total + product(q, p)
        q = core * s.nx + beside(2)
        for p, part in enumerate(s.parts):
            for k in range(2):
                lo, hi = ((0, part.half), (part.half, part.tb))[k]
                await_bytes(v.at[it, q, p, lo:hi], xg_rs.at[it, p, 2 + k])
                pass_mate(q, p, lo, hi, 3 + k)
            total = total + product(q, p)
        for d in (0, -1, 1, 2):
            q = other * s.nx + beside(d)
            for p, part in enumerate(s.parts):
                if d == 2:
                    await_bytes(v.at[it, q, p, 0 : part.half], cg_rs.at[it, p, 3])
                    await_bytes(v.at[it, q, p, part.half : part.tb], cg_rs.at[it, p, 4])
                else:
                    await_bytes(v.at[it, q, p, 0 : part.tb], cg_rs.at[it, p, (0, 2, 1)[d]])
                total = total + product(q, p)

        f_send[it, 0 : s.ft] = as_tiles(total).astype(BF16)
        if s.fz > s.ft:
            f_send[it, s.ft : s.fz] = jnp.zeros((s.fz - s.ft, TILE, LANE), BF16)
        for d in far_first(s.nz):
            piece = pl.ds(lax.rem(z + d, s.nz) * s.zp, s.zp)
            send(f_send.at[it, piece], f_recv.at[it, d - 1], z_ss.at[it], z_rs.at[it], along_z(d))

        def squares(q, running):
            for p, part in enumerate(s.parts):
                for j in range(part.blocks):
                    block = v[it, q, p, j * s.groups : (j + 1) * s.groups].astype(F32).reshape(n, LANE)
                    running = running + block * block
            return running

        running = lax.fori_loop(0, s.nq, squares, jnp.zeros((n, LANE), F32))
        sz_send[it] = to_row(jnp.sum(running, axis=1, keepdims=True))
        for d in far_first(s.nz):
            send(sz_send.at[it], sz_recv.at[it, d - 1], sz_ss.at[it], sz_rs.at[it], along_z(d))

        await_bytes(f_recv.at[it], z_rs.at[it])
        reduced = f_send[it, pl.ds(z * s.zp, s.zp)].astype(F32)
        for d in range(s.nz - 1):
            reduced = reduced + f_recv[it, d].astype(F32)
        mine = f_all.at[it, pl.ds(z * s.zp, s.zp)]
        mine[...] = reduced.astype(BF16)
        for d in far_first(s.nz):
            send(mine, mine, zg_ss.at[it], zg_rs.at[it], along_z(d))
        await_bytes(sz_recv.at[it], sz_rs.at[it])
        return from_row(sz_send[it] + jnp.sum(sz_recv[it], axis=0), n)

    def predicted(it):
        return [f_all[it, j * s.groups : (j + 1) * s.groups].astype(F32).reshape(n, LANE) for j in range(s.fb)]

    def gathered(it):
        await_bytes(f_recv.at[it], zg_rs.at[it])
        return predicted(it)

    adjoint(0, observed.astype(BF16), row_sums(lane_blocks(observed)))
    for p, part in enumerate(s.parts):
        share = y_share(0, p)
        spread_y(0, p, share)
        w1[p, 0 : part.tp] = share
    norm2 = forward(0)
    beta1 = jnp.sqrt(sum_end(0) + EPSILON)
    alpha1 = jnp.sqrt(norm2 / (beta1 * beta1) + EPSILON)
    scale1 = 1.0 / (beta1 * alpha1)
    ratio = alpha1 / beta1
    seen = lane_blocks(misfit[...])
    left = [f * scale1 - ratio * o for f, o in zip(gathered(0), seen, strict=True)]

    adjoint(1, jnp.concatenate(left, axis=1).astype(BF16), row_sums(left))
    beta2 = jnp.sqrt(sum_end(1) + EPSILON)
    coef[0] = (1.0 / beta2).reshape(s.groups, TILE, LANE)
    coef[1] = (beta2 * scale1).reshape(s.groups, TILE, LANE)
    for p, part in enumerate(s.parts):
        w2 = y_share(1, p)
        share = []
        for i in range(part.tp):
            group = lax.rem(y * part.tp + i, s.groups)
            share.append(w2[i] * coef[0, group] - w1[p, i] * coef[1, group])
        spread_y(1, p, jnp.stack(share, axis=0))
    norm2 = forward(1)
    alpha2 = jnp.sqrt(norm2 + EPSILON)
    inverse2 = 1.0 / alpha2
    ratio = alpha2 / beta2
    left = [f * inverse2 - ratio * o for f, o in zip(gathered(1), left, strict=True)]

    sum_start(2, row_sums(left))
    rho1 = jnp.sqrt(alpha1 * alpha1 + beta2 * beta2)
    cosine, sine = alpha1 / rho1, beta2 / rho1
    phi1 = cosine * beta1
    phibar = sine * beta1
    theta = sine * alpha2
    rhobar = -cosine * alpha2

    first = place * (s.width // s.rows)
    block = first // LANE
    lane = lax.rem(first, LANE)
    share_width = s.width // s.rows
    cover = -(-share_width // LANE)
    shape = ((cover + 1) * LANE, cover * LANE)
    pick = lax.broadcasted_iota(jnp.int32, shape, 0) == lax.broadcasted_iota(jnp.int32, shape, 1) + lane
    pick = jnp.where(pick, 1.0, 0.0).astype(BF16)
    window = []
    for it in range(2):
        sides = []
        for k in range(cover + 1):
            b = jnp.minimum(block + k, s.width // LANE - 1)
            j = lax.rem(b, s.nb)
            p = j // s.cut
            inside = (j - p * s.cut) * s.groups
            sides.append(v[it, b // s.nb, p, pl.ds(inside, s.groups)].reshape(n, LANE))
        window.append(jnp.dot(jnp.concatenate(sides, axis=1), pick, preferred_element_type=F32))

    sum_middle(2)
    beta3 = jnp.sqrt(sum_end(2) + EPSILON)
    rho2 = jnp.sqrt(rhobar * rhobar + beta3 * beta3)
    phi2 = rhobar / rho2 * phibar
    on2 = phi2 / rho2
    weight1 = (phi1 / rho1 - on2 * (theta / rho1)) * scale1
    weight2 = on2 * inverse2
    result = [weight1 * a + weight2 * b for a, b in zip(lane_blocks(window[0]), lane_blocks(window[1]), strict=True)]
    slip[...] = jnp.concatenate(result, axis=1)[:, 0:share_width]
    for j, (f1, f2, o) in enumerate(zip(predicted(0), predicted(1), seen, strict=True)):
        misfit[:, j * LANE : (j + 1) * LANE] = o - weight1 * f1 - weight2 * f2

    await_bytes(halo, halo_ss.at[0])
    for it in range(2):
        for p, part in enumerate(s.parts):
            four = pc_send.at[it, p, :, 0 : part.tb]
            three = px_send.at[it, p, :, 0 : part.tb]
            pieces = q_recv.at[it, p, :, 0 : part.tp]
            await_bytes(four, c_ss.at[it, p])
            await_bytes(three, x_ss.at[it, p])
            await_bytes(pieces, y_ss.at[it, p])
            await_bytes(pieces, yg_ss.at[it, p])
            await_bytes(three, xg_ss.at[it, p])
            await_bytes(four, cg_ss.at[it, p])
        await_bytes(f_recv.at[it], z_ss.at[it])
        await_bytes(f_recv.at[it], zg_ss.at[it])
        await_bytes(sz_recv.at[it], sz_ss.at[it])
    for i in range(3):
        await_bytes(sa_recv.at[i], sa_ss.at[i])
        await_bytes(sb_recv.at[i], sb_ss.at[i])


def body(dims, nz, data, source, near_tiles, near_rows, near_cols, near_count, far_left, far_right):
    realiz, pixels = data.shape
    rank, width = far_right.shape
    slots, tile_rows, tile_cols = near_tiles.shape
    s = Sizes(dims, nz, realiz, pixels, width, slots, rank, tile_rows, tile_cols)
    vmem = pl.BlockSpec(memory_space=pltpu.VMEM)
    return pl.pallas_call(
        functools.partial(kernel, s),
        out_shape=(
            jax.ShapeDtypeStruct((realiz, width // s.rows), F32),
            jax.ShapeDtypeStruct((realiz, pixels), F32),
        ),
        in_specs=[pl.BlockSpec(memory_space=pl.ANY)] * 8,
        out_specs=(vmem, vmem),
        scratch_shapes=scratch_shapes(s),
        compiler_params=pltpu.CompilerParams(
            collective_id=0, has_side_effects=True, vmem_limit_bytes=58 * 1024 * 1024
        ),
    )(
        data,
        source.reshape(1, pixels),
        near_rows.reshape(slots),
        near_cols.reshape(slots),
        near_count,
        near_tiles,
        far_left,
        far_right,
    )


def solution(mesh, dims=(4, 8, 2)):
    return jax.shard_map(
        functools.partial(body, dims, mesh.shape["cols"]),
        mesh=mesh,
        in_specs=(
            P(None, "rows"),
            P("rows"),
            P("rows", "cols", None),
            P("rows", "cols"),
            P("rows", "cols"),
            P("rows", "cols"),
            P("cols", "rows"),
            P("rows", "cols"),
        ),
        out_specs=(P(None, ("cols", "rows")), P(None, "rows")),
        check_vma=False,
    )
```

time: 111 us -> 109 us (0.982)
  local copies, waits for them, and re-layouts: 6.67 us -> 2.99 us
  Pallas kernels: 102 us -> 105 us
    unnamed x12 -> x2, local copies, waits for them, and re-layouts: 6.67 us -> 2.99 us
    pallas_call x1, Pallas kernels: 102 us -> 105 us  [body(): pl.pallas_call(functools.partial(kernel, s), out_shape=(jax.ShapeDtypeStr...]
where the time goes in v2:
time: 109 us
  Pallas kernels  105 us (96%)
  local copies, waits for them, and re-layouts  2.99 us (3%)
  between operations  1.29 us (1%)
    pallas_call x1, Pallas kernels, body(): pl.pallas_call(functools.partial(kernel, s), out_shape=(jax.ShapeDtypeStr...  105 us
    unnamed x2, local copies, waits for them, and re-layouts  2.99 us

profile of v2, /device:TPU:1, one launch (start us, length us, event | category | flops | bytes accessed | tf_op | source)
XLA Modules:
  0.0 109.1 jit_solution(18436969334846835899)
XLA Ops:
  1.3 104.8 %shard_map.95 = (f32[80,80]{1,0:T(8,128)}, f32[80,512]{1,0:T(8,128)}) custom-call(f32[80,512]{1,0:T(8,128)} %data_hbm.1, s32[1,512]{1,0:T(1,128)} %bitcast.3, s32[30]{0:T(128)} %bitcast.4, s32[30]{0:T(128)} %bitcast.5, s32[1,1]{1,0:T(1,128)S(6)} %copy.12.count_hbm, bf16[30,128,512]{2,1,0:T(8,128)(2,1)} %tiles_hbm.1, bf16[24,512]{1,0:T(8,128)(2,1)} %left_hbm.1, ...), custom_call_target="tpu_custom_call" | custom-call | tf_op jit(solution)/shard_map/pallas_call | solution.py:592
  106.1 1.4 %copy.13 = f32[80,80]{1,0:T(8,128)} copy(f32[80,80]{1,0:T(8,128)} %get-tuple-element.4) | data formatting | bytes 51200
  107.5 1.6 %copy.14 = f32[80,512]{1,0:T(8,128)} copy(f32[80,512]{1,0:T(8,128)} %get-tuple-element.5) | data formatting | bytes 327680

commit v3 on v2

v3 whole, which is shorter than its diff:
```python
import functools

import jax
import jax.numpy as jnp
from jax import lax
from jax.experimental import pallas as pl
from jax.experimental.pallas import tpu as pltpu
from jax.sharding import PartitionSpec as P

EPSILON = 1e-06
LANE = 128
TILE = 16
MESH = pl.DeviceIdType.MESH
F32 = jnp.float32
BF16 = jnp.bfloat16


class Part:
    def __init__(self, first, groups, s):
        self.first, self.groups = first, groups
        self.rows = slice(first * TILE, (first + groups) * TILE)
        self.n = groups * TILE
        self.tb = s.nb * groups
        self.tp = -(-self.tb // s.ny)
        self.tq = self.tp * s.ny
        self.half = (self.tb + 1) // 2
        self.ft = s.fb * groups
        self.zp = -(-self.ft // s.nz)
        self.fz = self.zp * s.nz


class Sizes:
    def __init__(self, dims, nz, realiz, pixels, width, slots, rank, tile_rows, tile_cols):
        self.nx, self.ny, self.cores = dims
        self.nz = nz
        self.rows = self.nx * self.ny * self.cores
        self.nq = self.nx * self.cores
        self.realiz, self.pixels, self.width = realiz, pixels, width
        self.slots, self.rank, self.tile_rows, self.tile_cols = slots, rank, tile_rows, tile_cols
        self.groups = realiz // TILE
        self.chunk = width // self.nq
        self.nb = self.chunk // LANE
        self.fb = pixels // LANE
        cut = (self.groups + 1) // 2
        self.parts = [Part(0, cut, self), Part(cut, self.groups - cut, self)]
        for name in ("tb", "tp", "tq", "zp", "fz"):
            setattr(self, name, max(getattr(p, name) for p in self.parts))


def scratch_shapes(s):
    dma = pltpu.SemaphoreType.DMA
    tile = (TILE, LANE)
    return [
        pltpu.VMEM((s.realiz, s.pixels), F32),
        pltpu.VMEM((1, s.pixels), jnp.int32),
        pltpu.VMEM((s.slots, s.tile_rows, s.tile_cols), BF16),
        pltpu.VMEM((s.rank, s.pixels), BF16),
        pltpu.VMEM((s.rank, s.width), BF16),
        pltpu.SMEM((s.slots,), jnp.int32),
        pltpu.SMEM((s.slots,), jnp.int32),
        pltpu.SMEM((1, 1), jnp.int32),
        pltpu.VMEM((8, LANE), jnp.int32),
        pltpu.SMEM((8, LANE), jnp.int32),
        pltpu.VMEM((2, s.realiz, s.pixels), F32),
        pltpu.VMEM((3, s.pixels, s.pixels), BF16),
        pltpu.VMEM((s.nq, s.pixels, s.chunk), BF16),
        pltpu.VMEM((2, 2, s.nx, s.tb, *tile), BF16),
        pltpu.VMEM((2, 2, s.nx, s.tb, *tile), BF16),
        pltpu.VMEM((2, 2, 3, s.tb, *tile), BF16),
        pltpu.VMEM((2, 2, 3, s.tb, *tile), BF16),
        pltpu.VMEM((2, 2, s.tq, *tile), BF16),
        pltpu.VMEM((2, 2, s.ny - 1, s.tp, *tile), BF16),
        pltpu.VMEM((2, s.nq, 2, s.tq, *tile), BF16),
        pltpu.VMEM((2, 2, s.fz, *tile), BF16),
        pltpu.VMEM((2, 2, s.nz - 1, s.zp, *tile), BF16),
        pltpu.VMEM((2, 2, s.fz, *tile), BF16),
        pltpu.VMEM((s.realiz, s.pixels), F32),
        pltpu.VMEM((2, s.realiz, LANE), F32),
        pltpu.VMEM((2, s.realiz, LANE), F32),
        pltpu.VMEM((s.realiz, LANE), F32),
        pltpu.VMEM((2, s.tp, *tile), F32),
        pltpu.VMEM((2, s.groups, *tile), F32),
        pltpu.VMEM((3, 8, LANE), F32),
        pltpu.VMEM((3, s.nq - 1, 8, LANE), F32),
        pltpu.VMEM((3, 8, LANE), F32),
        pltpu.VMEM((3, s.ny - 1, 8, LANE), F32),
        pltpu.VMEM((2, 8, LANE), F32),
        pltpu.VMEM((2, s.nz - 1, 8, LANE), F32),
        dma((9,)),
        dma((1,)),
        dma((2,)),
        dma((2, 2)),
        dma((2, 2, s.nx)),
        dma((2, 2)),
        dma((2, 2, 4)),
        dma((2, 2)),
        dma((2, 2)),
        dma((2, 2)),
        dma((2, 2)),
        dma((2, 2)),
        dma((2, 2, 4)),
        dma((2, 2)),
        dma((2, 2, 5)),
        dma((2, 2)),
        dma((2, 2)),
        dma((2, 2)),
        dma((2, 2)),
        dma((3,)),
        dma((3,)),
        dma((3,)),
        dma((3,)),
        dma((2,)),
        dma((2,)),
    ]


def far_first(count):
    return sorted(range(1, count), key=lambda d: (-min(d, count - d), d))


def near_first(count):
    return sorted(range(1, count), key=lambda d: (min(d, count - d), d))


def await_bytes(ref, sem):
    pltpu.make_async_copy(ref, ref, sem).wait()


def to_row(column):
    rows = column.shape[0]
    wide = jnp.broadcast_to(column, (rows, LANE))
    wide = jnp.concatenate([wide, jnp.zeros((LANE - rows, LANE), F32)], axis=0)
    return wide.T[0:8]


def from_row(row, rows):
    return jnp.broadcast_to(row[0:1], (LANE, LANE)).T[0:rows]


def row_sums(blocks):
    total = blocks[0] * blocks[0]
    for block in blocks[1:]:
        total = total + block * block
    return jnp.sum(total, axis=1, keepdims=True)


def lane_blocks(value):
    return [value[:, j * LANE : (j + 1) * LANE] for j in range(value.shape[1] // LANE)]


def as_tiles(value):
    groups = value.shape[0] // TILE
    return jnp.concatenate([b.reshape(groups, TILE, LANE) for b in lane_blocks(value)], axis=0)


def from_tiles(tiles, groups):
    count = tiles.shape[0] // groups
    return jnp.concatenate(
        [tiles[j * groups : (j + 1) * groups].reshape(groups * TILE, LANE) for j in range(count)], axis=1
    )


def three_parts(value):
    high = value.astype(BF16)
    rest = value - high.astype(F32)
    middle = rest.astype(BF16)
    low = (rest - middle.astype(F32)).astype(BF16)
    return jnp.concatenate([high, middle, low], axis=0)


def kernel(
    s, data_hbm, source_hbm, rows_hbm, cols_hbm, count_hbm, tiles_hbm, left_hbm, right_hbm, slip, misfit,
    data, source, tiles, far_left, far_right, near_rows, near_cols, near_count, table, table_s, halo, onehot, g,
    pc_send, pc_recv, px_send, px_recv, q_send, q_recv, v, f_send, f_recv, f_all, left, alphas, betas, inverse,
    previous, coef, sa_send, sa_recv, sb_send, sb_recv, sz_send, sz_recv, in_sem, halo_ss, halo_rs, c_ss, c_rs,
    x_ss, x_rs, y_ss, y_rs, yg_ss, yg_rs, xg_ss, xg_rs, cg_ss, cg_rs, z_ss, z_rs, zg_ss, zg_rs, sa_ss, sa_rs,
    sb_ss, sb_rs, sz_ss, sz_rs,
):
    place = lax.axis_index("rows")
    z = lax.axis_index("cols")
    core = lax.rem(place, 2)
    chip = place // 2
    y = lax.rem(chip, s.ny)
    x = chip // s.ny
    other = 1 - core
    own_q = core * s.nx + x
    n = s.realiz

    def at(xx, yy, cc):
        return ((xx * s.ny + yy) * 2 + cc, z)

    def cross(d):
        q = lax.rem(own_q + d, s.nq)
        return at(lax.rem(q, s.nx), y, q // s.nx)

    def along_y(d):
        return at(x, lax.rem(y + d, s.ny), core)

    def along_z(d):
        return (place, lax.rem(z + d, s.nz))

    def beside(d):
        return lax.rem(x + d + s.nx, s.nx)

    mate = at(x, y, other)
    up = at(beside(1), y, core)
    down = at(beside(-1), y, core)

    def send(src, dst, send_sem, recv_sem, device):
        pltpu.make_async_remote_copy(
            src_ref=src, dst_ref=dst, send_sem=send_sem, recv_sem=recv_sem, device_id=device, device_id_type=MESH
        ).start()

    pairs = [
        (rows_hbm, near_rows),
        (cols_hbm, near_cols),
        (count_hbm, near_count),
        (source_hbm, source),
        (data_hbm, data),
        (left_hbm, far_left),
        (right_hbm, far_right),
        (tiles_hbm, tiles),
    ]
    loads = [pltpu.make_async_copy(src, dst, in_sem.at[k]) for k, (src, dst) in enumerate(pairs)]
    for load in loads:
        load.start()

    step_out = lax.rem(place + s.rows + 2 * core - 1, s.rows)
    partners = [cross(d) for d in range(1, s.nq)]
    partners += [along_y(d) for d in range(1, s.ny)]
    partners += [along_z(d) for d in range(1, s.nz)]
    partners += [(step_out, z)]
    barrier = pltpu.get_barrier_semaphore()
    for device in partners:
        pl.semaphore_signal(barrier, inc=1, device_id=device, device_id_type=MESH)

    for load in loads[:3]:
        load.wait()
    per_row = s.width // s.tile_cols
    spot = lax.broadcasted_iota(jnp.int32, (8, LANE), 1)
    slot_of = jnp.full((8, LANE), -1, jnp.int32)
    for k in range(s.slots):
        where = jnp.where(k < near_count[0, 0], near_rows[k] * per_row + near_cols[k], -1)
        slot_of = jnp.where(spot == where, k, slot_of)
    table[...] = slot_of
    to_scalars = pltpu.make_async_copy(table, table_s, in_sem.at[8])
    to_scalars.start()

    pl.semaphore_wait(barrier, len(partners))

    after = lax.rem(place + 1, s.rows)
    before = lax.rem(place + s.rows - 1, s.rows)
    loads[4].wait()
    send(data, halo.at[0], halo_ss.at[0], halo_rs.at[0], (after, z))
    send(data, halo.at[1], halo_ss.at[0], halo_rs.at[1], (before, z))

    loads[3].wait()
    total = s.rows * s.pixels
    offset = source[...] + s.pixels - place * s.pixels
    offset = jnp.where(offset < 0, offset + total, offset)
    offset = jnp.where(offset >= total, offset - total, offset)
    index = lax.broadcasted_iota(jnp.int32, (s.pixels, s.pixels), 0)
    for k in range(3):
        onehot[k] = jnp.where(index == offset - k * s.pixels, 1.0, 0.0).astype(BF16)

    for load in loads[5:]:
        load.wait()
    to_scalars.wait()
    half = per_row // 2
    half_blocks = half * s.tile_cols // LANE
    bands = s.pixels // s.tile_rows

    def build(i, carry):
        side, a = i // bands, lax.rem(i, bands)
        pixel = pl.ds(pl.multiple_of(a * s.tile_rows, s.tile_rows), s.tile_rows)
        lefts = far_left[:, pixel]
        for b in range(half):
            column = pl.ds(pl.multiple_of((side * half + b) * s.tile_cols, s.tile_cols), s.tile_cols)
            block = lax.dot_general(lefts, far_right[:, column], (((0,), (0,)), ((), ())), preferred_element_type=F32)
            slot = table_s[0, a * per_row + side * half + b]
            near = tiles[jnp.maximum(slot, 0)].astype(F32)
            block = (block + near * jnp.where(slot >= 0, 1.0, 0.0)).astype(BF16)
            for k in range(s.tile_cols // LANE):
                j = b * (s.tile_cols // LANE) + k
                q = side * (half_blocks // s.nb) + j // s.nb
                lane = (j % s.nb) * LANE
                g[q, pixel, lane : lane + LANE] = block[:, k * LANE : (k + 1) * LANE]
        return carry

    lax.fori_loop(0, 2 * bands, build, 0)

    seen = jnp.dot(three_parts(data[...]), onehot[1], preferred_element_type=F32)
    for k in range(2):
        await_bytes(halo.at[k], halo_rs.at[k])
        seen = seen + jnp.dot(three_parts(halo[k]), onehot[2 * k], preferred_element_type=F32)
    observed = (seen[0:n] + seen[n : 2 * n]) + seen[2 * n : 3 * n]
    misfit[...] = observed
    left[...] = observed
    previous[...] = jnp.zeros_like(previous)
    inverse[...] = jnp.zeros_like(inverse)

    def sum_start(i, column):
        sa_send[i] = to_row(column)
        for d in range(1, s.nq):
            send(sa_send.at[i], sa_recv.at[i, d - 1], sa_ss.at[i], sa_rs.at[i], cross(d))

    def sum_middle(i):
        await_bytes(sa_recv.at[i], sa_rs.at[i])
        sb_send[i] = sa_send[i] + jnp.sum(sa_recv[i], axis=0)
        for d in range(1, s.ny):
            send(sb_send.at[i], sb_recv.at[i, d - 1], sb_ss.at[i], sb_rs.at[i], along_y(d))

    def sum_end(i):
        await_bytes(sb_recv.at[i], sb_rs.at[i])
        return jnp.sqrt(from_row(sb_send[i] + jnp.sum(sb_recv[i], axis=0), n) + EPSILON)

    def pieces_of(p):
        return ((0, s.parts[p].half), (s.parts[p].half, s.parts[p].tb))

    def product(p, q):
        return as_tiles(jnp.dot(left[s.parts[p].rows, :].astype(BF16), g[q], preferred_element_type=F32))

    def to_mate(it, p):
        tb = s.parts[p].tb
        for d in (2, 1, 3, 0):
            mine = pc_send.at[it, p, d, 0:tb]
            mine[...] = product(p, other * s.nx + beside(d)).astype(BF16)
            send(mine, pc_recv.at[it, p, d, 0:tb], c_ss.at[it, p], c_rs.at[it, p, d], mate)

    def pair_sum(it, p, d):
        own = product(p, core * s.nx + beside(d))
        came = pc_recv.at[it, p, d, 0 : s.parts[p].tb]
        await_bytes(came, c_rs.at[it, p, d])
        return own + came[...].astype(F32)

    def relay_out(it, p):
        px_send[it, p, 0, 0 : s.parts[p].tb] = pair_sum(it, p, 2).astype(BF16)
        for k, (lo, hi) in enumerate(pieces_of(p)):
            send(
                px_send.at[it, p, 0, lo:hi],
                px_recv.at[it, p, 2, lo:hi],
                x_ss.at[it, p],
                x_rs.at[it, p, 2 + k],
                (up, down)[k],
            )

    def relay_on(it, p):
        tb = s.parts[p].tb
        for k, (lo, hi) in enumerate(pieces_of(p)):
            own = pair_sum(it, p, (1, 3)[k])
            came = px_recv.at[it, p, 2, lo:hi]
            await_bytes(came, x_rs.at[it, p, 2 + k])
            passed = own[lo:hi] + came[...].astype(F32)
            own = jnp.concatenate([passed, own[hi:]] if k == 0 else [own[:lo], passed], axis=0)
            px_send[it, p, 1 + k, 0:tb] = own.astype(BF16)
            send(
                px_send.at[it, p, 1 + k, 0:tb],
                px_recv.at[it, p, k, 0:tb],
                x_ss.at[it, p],
                x_rs.at[it, p, k],
                (up, down)[k],
            )

    def scatter_y(it, p):
        tb, tp, tq = s.parts[p].tb, s.parts[p].tp, s.parts[p].tq
        own = pair_sum(it, p, 0)
        for k in range(2):
            came = px_recv.at[it, p, k, 0:tb]
            await_bytes(came, x_rs.at[it, p, k])
            own = own + came[...].astype(F32)
        q_send[it, p, 0:tb] = own.astype(BF16)
        if tq > tb:
            q_send[it, p, tb:tq] = jnp.zeros((tq - tb, TILE, LANE), BF16)
        for d in far_first(s.ny):
            piece = pl.ds(lax.rem(y + d, s.ny) * tp, tp)
            send(q_send.at[it, p, piece], q_recv.at[it, p, d - 1, 0:tp], y_ss.at[it, p], y_rs.at[it, p], along_y(d))

    def spread_y(it, p):
        tp = s.parts[p].tp
        await_bytes(q_recv.at[it, p, :, 0:tp], y_rs.at[it, p])
        share = q_send[it, p, pl.ds(y * tp, tp)].astype(F32)
        for d in range(s.ny - 1):
            share = share + q_recv[it, p, d, 0:tp].astype(F32)
        mine = v.at[it, own_q, p, pl.ds(y * tp, tp)]
        for i in range(tp):
            group = s.parts[p].first + lax.rem(y * tp + i, s.parts[p].groups)
            raw = share[i] * coef[0, group] - previous[p, i] * coef[1, group]
            previous[p, i] = raw
            v[it, own_q, p, y * tp + i] = raw.astype(BF16)
        for d in far_first(s.ny):
            send(mine, mine, yg_ss.at[it, p], yg_rs.at[it, p], along_y(d))

    def applied(it, p, q):
        return lax.dot_general(
            from_tiles(v[it, q, p, 0 : s.parts[p].tb], s.parts[p].groups),
            g[q],
            (((1,), (1,)), ((), ())),
            preferred_element_type=F32,
        )

    def pass_x(it, p, q, lo, hi, k, device):
        piece = v.at[it, q, p, lo:hi]
        send(piece, piece, xg_ss.at[it, p], xg_rs.at[it, p, k], device)

    def pass_mate(it, p, q, lo, hi, k):
        piece = v.at[it, q, p, lo:hi]
        send(piece, piece, cg_ss.at[it, p], cg_rs.at[it, p, k], mate)

    def own_chunk(it, p):
        part = s.parts[p]
        await_bytes(q_recv.at[it, p, :, 0 : part.tp], yg_rs.at[it, p])
        pass_x(it, p, own_q, 0, part.tb, 0, up)
        pass_x(it, p, own_q, 0, part.tb, 1, down)
        pass_mate(it, p, own_q, 0, part.tb, 0)
        return applied(it, p, own_q)

    def next_chunks(it, p, total):
        part = s.parts[p]
        for k, (lo, hi) in enumerate(pieces_of(p)):
            q = core * s.nx + beside((-1, 1)[k])
            await_bytes(v.at[it, q, p, 0 : part.tb], xg_rs.at[it, p, k])
            pass_x(it, p, q, lo, hi, 2 + k, (up, down)[k])
            pass_mate(it, p, q, 0, part.tb, 1 + k)
        for d in (-1, 1):
            total = total + applied(it, p, core * s.nx + beside(d))
        q = other * s.nx + x
        await_bytes(v.at[it, q, p, 0 : part.tb], cg_rs.at[it, p, 0])
        return total + applied(it, p, q)

    def far_chunk(it, p, total):
        q = core * s.nx + beside(2)
        for k, (lo, hi) in enumerate(pieces_of(p)):
            await_bytes(v.at[it, q, p, lo:hi], xg_rs.at[it, p, 2 + k])
            pass_mate(it, p, q, lo, hi, 3 + k)
        total = total + applied(it, p, q)
        for d in (-1, 1):
            q = other * s.nx + beside(d)
            await_bytes(v.at[it, q, p, 0 : s.parts[p].tb], cg_rs.at[it, p, (0, 2, 1)[d]])
            total = total + applied(it, p, q)
        return total

    def scatter_z(it, p, total):
        part = s.parts[p]
        q = other * s.nx + beside(2)
        for k, (lo, hi) in enumerate(pieces_of(p)):
            await_bytes(v.at[it, q, p, lo:hi], cg_rs.at[it, p, 3 + k])
        total = total + applied(it, p, q)
        f_send[it, p, 0 : part.ft] = as_tiles(total).astype(BF16)
        if part.fz > part.ft:
            f_send[it, p, part.ft : part.fz] = jnp.zeros((part.fz - part.ft, TILE, LANE), BF16)
        for d in far_first(s.nz):
            piece = pl.ds(lax.rem(z + d, s.nz) * part.zp, part.zp)
            send(
                f_send.at[it, p, piece],
                f_recv.at[it, p, d - 1, 0 : part.zp],
                z_ss.at[it, p],
                z_rs.at[it, p],
                along_z(d),
            )

    def spread_z(it, p):
        zp = s.parts[p].zp
        await_bytes(f_recv.at[it, p, :, 0:zp], z_rs.at[it, p])
        reduced = f_send[it, p, pl.ds(z * zp, zp)].astype(F32)
        for d in range(s.nz - 1):
            reduced = reduced + f_recv[it, p, d, 0:zp].astype(F32)
        mine = f_all.at[it, p, pl.ds(z * zp, zp)]
        mine[...] = reduced.astype(BF16)
        for d in far_first(s.nz):
            send(mine, mine, zg_ss.at[it, p], zg_rs.at[it, p], along_z(d))

    def square_sums(it):
        sums = []
        for p, part in enumerate(s.parts):

            def squares(q, running, p=p, part=part):
                for j in range(s.nb):
                    block = v[it, q, p, j * part.groups : (j + 1) * part.groups].astype(F32).reshape(part.n, LANE)
                    running = running + block * block
                return running

            running = lax.fori_loop(0, s.nq, squares, jnp.zeros((part.n, LANE), F32))
            sums.append(jnp.sum(running, axis=1, keepdims=True))
        return jnp.concatenate(sums, axis=0)

    def predicted(it, p, j):
        part = s.parts[p]
        return f_all[it, p, j * part.groups : (j + 1) * part.groups].astype(F32).reshape(part.n, LANE)

    def left_sums():
        return row_sums(lane_blocks(left[...]))

    both = range(2)

    def iteration(it, carry):
        to_mate(it, 0)
        sum_start(it, left_sums())
        to_mate(it, 1)
        for p in both:
            relay_out(it, p)
        for p in both:
            relay_on(it, p)
        sum_middle(it)
        for p in both:
            scatter_y(it, p)
        beta = sum_end(it)
        betas[it] = beta
        coef[0] = (1.0 / beta).reshape(s.groups, TILE, LANE)
        coef[1] = (beta * inverse[...]).reshape(s.groups, TILE, LANE)
        for p in both:
            spread_y(it, p)
        total = [own_chunk(it, p) for p in both]
        total = [next_chunks(it, p, total[p]) for p in both]
        total = [far_chunk(it, p, total[p]) for p in both]
        for p in both:
            scatter_z(it, p, total[p])
        sz_send[it] = to_row(square_sums(it))
        for d in far_first(s.nz):
            send(sz_send.at[it], sz_recv.at[it, d - 1], sz_ss.at[it], sz_rs.at[it], along_z(d))
        for p in both:
            spread_z(it, p)
        await_bytes(sz_recv.at[it], sz_rs.at[it])
        alpha = jnp.sqrt(from_row(sz_send[it] + jnp.sum(sz_recv[it], axis=0), n) + EPSILON)
        alphas[it] = alpha
        inverse[...] = 1.0 / alpha
        ratio = alpha / beta
        for p, part in enumerate(s.parts):
            await_bytes(f_recv.at[it, p, :, 0 : part.zp], zg_rs.at[it, p])
            for j in range(s.fb):
                lanes = slice(j * LANE, (j + 1) * LANE)
                left[part.rows, lanes] = (
                    predicted(it, p, j) * inverse[part.rows] - left[part.rows, lanes] * ratio[part.rows]
                )
        return carry

    lax.fori_loop(0, 2, iteration, 0)

    sum_start(2, left_sums())
    alpha1, alpha2, beta1, beta2 = alphas[0], alphas[1], betas[0], betas[1]
    rho1 = jnp.sqrt(alpha1 * alpha1 + beta2 * beta2)
    cosine, sine = alpha1 / rho1, beta2 / rho1
    phi1 = cosine * beta1
    phibar = sine * beta1
    theta = sine * alpha2
    rhobar = -cosine * alpha2

    first = place * (s.width // s.rows)
    block = first // LANE
    lane = lax.rem(first, LANE)
    share_width = s.width // s.rows
    cover = -(-share_width // LANE)
    shape = ((cover + 1) * LANE, cover * LANE)
    pick = lax.broadcasted_iota(jnp.int32, shape, 0) == lax.broadcasted_iota(jnp.int32, shape, 1) + lane
    pick = jnp.where(pick, 1.0, 0.0).astype(BF16)
    window = []
    for it in range(2):
        sides = []
        for k in range(cover + 1):
            b = jnp.minimum(block + k, s.width // LANE - 1)
            j = lax.rem(b, s.nb)
            rows = [
                v[it, b // s.nb, p, pl.ds(j * part.groups, part.groups)].reshape(part.n, LANE)
                for p, part in enumerate(s.parts)
            ]
            sides.append(jnp.concatenate(rows, axis=0))
        window.append(jnp.dot(jnp.concatenate(sides, axis=1), pick, preferred_element_type=F32))

    sum_middle(2)
    beta3 = sum_end(2)
    rho2 = jnp.sqrt(rhobar * rhobar + beta3 * beta3)
    phi2 = rhobar / rho2 * phibar
    on2 = phi2 / rho2
    weight1 = (phi1 / rho1 - on2 * (theta / rho1)) / alpha1
    weight2 = on2 / alpha2
    result = [weight1 * a + weight2 * b for a, b in zip(lane_blocks(window[0]), lane_blocks(window[1]), strict=True)]
    slip[...] = jnp.concatenate(result, axis=1)[:, 0:share_width]
    for p, part in enumerate(s.parts):
        for j in range(s.fb):
            lanes = slice(j * LANE, (j + 1) * LANE)
            misfit[part.rows, lanes] = (
                misfit[part.rows, lanes]
                - weight1[part.rows] * predicted(0, p, j)
                - weight2[part.rows] * predicted(1, p, j)
            )

    await_bytes(halo, halo_ss.at[0])

    def settle(it, carry):
        for p, part in enumerate(s.parts):
            four = pc_send.at[it, p, :, 0 : part.tb]
            three = px_send.at[it, p, :, 0 : part.tb]
            pieces = q_recv.at[it, p, :, 0 : part.tp]
            fields = f_recv.at[it, p, :, 0 : part.zp]
            await_bytes(four, c_ss.at[it, p])
            await_bytes(three, x_ss.at[it, p])
            await_bytes(pieces, y_ss.at[it, p])
            await_bytes(pieces, yg_ss.at[it, p])
            await_bytes(three, xg_ss.at[it, p])
            await_bytes(four, cg_ss.at[it, p])
            await_bytes(fields, z_ss.at[it, p])
            await_bytes(fields, zg_ss.at[it, p])
        await_bytes(sz_recv.at[it], sz_ss.at[it])
        return carry

    lax.fori_loop(0, 2, settle, 0)
    for i in range(3):
        await_bytes(sa_recv.at[i], sa_ss.at[i])
        await_bytes(sb_recv.at[i], sb_ss.at[i])


def hand_over(slip_in, misfit_in, slip_out, misfit_out, sem):
    copies = [
        pltpu.make_async_copy(slip_in, slip_out, sem.at[0]),
        pltpu.make_async_copy(misfit_in, misfit_out, sem.at[1]),
    ]
    for copy in copies:
        copy.start()
    for copy in copies:
        copy.wait()


def body(dims, nz, data, source, near_tiles, near_rows, near_cols, near_count, far_left, far_right):
    realiz, pixels = data.shape
    rank, width = far_right.shape
    slots, tile_rows, tile_cols = near_tiles.shape
    s = Sizes(dims, nz, realiz, pixels, width, slots, rank, tile_rows, tile_cols)
    vmem = pl.BlockSpec(memory_space=pltpu.VMEM)
    out_shape = (
        jax.ShapeDtypeStruct((realiz, width // s.rows), F32),
        jax.ShapeDtypeStruct((realiz, pixels), F32),
    )
    results = pl.pallas_call(
        functools.partial(kernel, s),
        out_shape=out_shape,
        in_specs=[pl.BlockSpec(memory_space=pl.ANY)] * 8,
        out_specs=(vmem, vmem),
        scratch_shapes=scratch_shapes(s),
        compiler_params=pltpu.CompilerParams(
            collective_id=0, has_side_effects=True, vmem_limit_bytes=58 * 1024 * 1024
        ),
    )(
        data,
        source.reshape(1, pixels),
        near_rows.reshape(slots),
        near_cols.reshape(slots),
        near_count,
        near_tiles,
        far_left,
        far_right,
    )
    anywhere = pl.BlockSpec(memory_space=pl.ANY)
    return pl.pallas_call(
        hand_over,
        out_shape=out_shape,
        in_specs=[anywhere] * 2,
        out_specs=(anywhere, anywhere),
        scratch_shapes=[pltpu.SemaphoreType.DMA((2,))],
        compiler_params=pltpu.CompilerParams(vmem_limit_bytes=58 * 1024 * 1024),
    )(*results)


def solution(mesh, dims=(4, 8, 2)):
    return jax.shard_map(
        functools.partial(body, dims, mesh.shape["cols"]),
        mesh=mesh,
        in_specs=(
            P(None, "rows"),
            P("rows"),
            P("rows", "cols", None),
            P("rows", "cols"),
            P("rows", "cols"),
            P("rows", "cols"),
            P("cols", "rows"),
            P("rows", "cols"),
        ),
        out_specs=(P(None, ("cols", "rows")), P(None, "rows")),
        check_vma=False,
    )
```

time: 109 us -> 115 us (1.055)
  Pallas kernels: 105 us -> 114 us
  local copies, waits for them, and re-layouts: 2.99 us -> 0 us
    pallas_call x1 -> x2, Pallas kernels: 105 us -> 114 us  [the longest x1 106 us: body(): pl.pallas_call(functools.partial(kernel, s), out_shape=out_shape, in_spec...]
    unnamed x2 -> x0, local copies, waits for them, and re-layouts: 2.99 us -> none
where the time goes in v3:
time: 115 us
  Pallas kernels  114 us (99%)
  between operations  1.29 us (1%)
    pallas_call x1, Pallas kernels, body(): pl.pallas_call(functools.partial(kernel, s), out_shape=out_shape, in_spec...  106 us
    pallas_call x1, Pallas kernels, body(): pl.pallas_call(hand_over, out_shape=out_shape, in_specs=[anywhere] * 2, o...  7.32 us

profile of v3, /device:TPU:1, one launch (start us, length us, event | category | flops | bytes accessed | tf_op | source)
XLA Modules:
  0.0 114.9 jit_solution(2727565885025967356)
XLA Ops:
  1.3 106.3 %shard_map.95 = (f32[80,80]{1,0:T(8,128)}, f32[80,512]{1,0:T(8,128)}) custom-call(f32[80,512]{1,0:T(8,128)} %data_hbm.1, s32[1,512]{1,0:T(1,128)} %bitcast.3, s32[30]{0:T(128)} %bitcast.4, s32[30]{0:T(128)} %bitcast.5, s32[1,1]{1,0:T(1,128)S(6)} %copy.10.count_hbm, bf16[30,128,512]{2,1,0:T(8,128)(2,1)} %tiles_hbm.1, bf16[24,512]{1,0:T(8,128)(2,1)} %left_hbm.1, ...), custom_call_target="tpu_custom_call" | custom-call | tf_op jit(solution)/shard_map/pallas_call | solution.py:632
  107.6 7.3 %shard_map.96 = (f32[80,80]{1,0:T(8,128)}, f32[80,512]{1,0:T(8,128)}) custom-call(f32[80,80]{1,0:T(8,128)} %get-tuple-element.4.slip_in, f32[80,512]{1,0:T(8,128)} %get-tuple-element.5.misfit_in), custom_call_target="tpu_custom_call" | custom-call | tf_op jit(solution)/shard_map/pallas_call | solution.py:652

commit v4 on v2

v4 whole, which is shorter than its diff:
```python
import functools

import jax
import jax.numpy as jnp
from jax import lax
from jax.experimental import pallas as pl
from jax.experimental.pallas import tpu as pltpu
from jax.sharding import PartitionSpec as P

EPSILON = 1e-06
LANE = 128
TILE = 16
MESH = pl.DeviceIdType.MESH
F32 = jnp.float32
BF16 = jnp.bfloat16


class Part:
    def __init__(self, first, blocks, s):
        self.lanes = slice(first * LANE, (first + blocks) * LANE)
        self.blocks = blocks
        self.tb = blocks * s.groups
        self.tp = -(-self.tb // s.ny)
        self.tq = self.tp * s.ny


class Sizes:
    def __init__(self, dims, nz, realiz, pixels, width, slots, rank, tile_rows, tile_cols):
        self.nx, self.ny, self.cores = dims
        self.nz = nz
        self.rows = self.nx * self.ny * self.cores
        self.nq = self.nx * self.cores
        self.realiz, self.pixels, self.width = realiz, pixels, width
        self.slots, self.rank, self.tile_rows, self.tile_cols = slots, rank, tile_rows, tile_cols
        self.groups = realiz // TILE
        self.chunk = width // self.nq
        self.nb = self.chunk // LANE
        self.fb = pixels // LANE
        self.ft = self.fb * self.groups
        self.zp = -(-self.ft // nz)
        self.fz = self.zp * nz
        self.cut = (self.nb + 1) // 2
        self.parts = [Part(0, self.cut, self), Part(self.cut, self.nb - self.cut, self)]
        self.tb = max(p.tb for p in self.parts)
        self.tp = max(p.tp for p in self.parts)
        self.tq = max(p.tq for p in self.parts)


def scratch_shapes(s):
    dma = pltpu.SemaphoreType.DMA
    tile = (TILE, LANE)
    return [
        pltpu.VMEM((s.realiz, s.pixels), F32),
        pltpu.VMEM((1, s.pixels), jnp.int32),
        pltpu.VMEM((s.slots, s.tile_rows, s.tile_cols), BF16),
        pltpu.VMEM((s.rank, s.pixels), BF16),
        pltpu.VMEM((s.rank, s.width), BF16),
        pltpu.SMEM((s.slots,), jnp.int32),
        pltpu.SMEM((s.slots,), jnp.int32),
        pltpu.SMEM((1, 1), jnp.int32),
        pltpu.VMEM((8, LANE), jnp.int32),
        pltpu.SMEM((8, LANE), jnp.int32),
        pltpu.VMEM((2, s.realiz, s.pixels), F32),
        pltpu.VMEM((3, s.pixels, s.pixels), BF16),
        pltpu.VMEM((s.nq, s.pixels, s.chunk), BF16),
        pltpu.VMEM((2, 2, s.nx, s.tb, *tile), BF16),
        pltpu.VMEM((2, 2, s.nx, s.tb, *tile), BF16),
        pltpu.VMEM((2, 2, s.nx - 1, s.tb, *tile), BF16),
        pltpu.VMEM((2, 2, s.nx - 1, s.tb, *tile), BF16),
        pltpu.VMEM((2, 2, s.tq, *tile), BF16),
        pltpu.VMEM((2, 2, s.ny - 1, s.tp, *tile), BF16),
        pltpu.VMEM((2, s.nq, 2, s.tq, *tile), BF16),
        pltpu.VMEM((2, s.fz, *tile), BF16),
        pltpu.VMEM((2, s.nz - 1, s.zp, *tile), BF16),
        pltpu.VMEM((2, s.fz, *tile), BF16),
        pltpu.VMEM((s.realiz, s.pixels), F32),
        pltpu.VMEM((2, s.realiz, LANE), F32),
        pltpu.VMEM((2, s.realiz, LANE), F32),
        pltpu.VMEM((s.realiz, LANE), F32),
        pltpu.VMEM((2, s.tp, *tile), F32),
        pltpu.VMEM((2, s.groups, *tile), F32),
        pltpu.VMEM((3, 8, LANE), F32),
        pltpu.VMEM((3, s.nq - 1, 8, LANE), F32),
        pltpu.VMEM((3, 8, LANE), F32),
        pltpu.VMEM((3, s.ny - 1, 8, LANE), F32),
        pltpu.VMEM((2, 8, LANE), F32),
        pltpu.VMEM((2, s.nz - 1, 8, LANE), F32),
        dma((9,)),
        dma((1,)),
        dma((2,)),
        dma((2, 2)),
        dma((2, 2, s.nx)),
        dma((2, 2)),
        dma((2, 2, s.nx - 1)),
        dma((2, 2)),
        dma((2, 2)),
        dma((2, 2)),
        dma((2, 2)),
        dma((2, 2)),
        dma((2, 2, s.nx - 1)),
        dma((2, 2)),
        dma((2, 2, s.nx)),
        dma((2,)),
        dma((2,)),
        dma((2,)),
        dma((2,)),
        dma((3,)),
        dma((3,)),
        dma((3,)),
        dma((3,)),
        dma((2,)),
        dma((2,)),
    ]


def far_first(count):
    return sorted(range(1, count), key=lambda d: (-min(d, count - d), d))


def near_first(count):
    return sorted(range(1, count), key=lambda d: (min(d, count - d), d))


def await_bytes(ref, sem):
    pltpu.make_async_copy(ref, ref, sem).wait()


def to_row(column):
    rows = column.shape[0]
    wide = jnp.broadcast_to(column, (rows, LANE))
    wide = jnp.concatenate([wide, jnp.zeros((LANE - rows, LANE), F32)], axis=0)
    return wide.T[0:8]


def from_row(row, rows):
    return jnp.broadcast_to(row[0:1], (LANE, LANE)).T[0:rows]


def row_sums(blocks):
    total = blocks[0] * blocks[0]
    for block in blocks[1:]:
        total = total + block * block
    return jnp.sum(total, axis=1, keepdims=True)


def lane_blocks(value):
    return [value[:, j * LANE : (j + 1) * LANE] for j in range(value.shape[1] // LANE)]


def as_tiles(value):
    groups = value.shape[0] // TILE
    return jnp.concatenate([b.reshape(groups, TILE, LANE) for b in lane_blocks(value)], axis=0)


def from_tiles(tiles, groups):
    count = tiles.shape[0] // groups
    return jnp.concatenate(
        [tiles[j * groups : (j + 1) * groups].reshape(groups * TILE, LANE) for j in range(count)], axis=1
    )


def three_parts(value):
    high = value.astype(BF16)
    rest = value - high.astype(F32)
    middle = rest.astype(BF16)
    low = (rest - middle.astype(F32)).astype(BF16)
    return jnp.concatenate([high, middle, low], axis=0)


def kernel(
    s, data_hbm, source_hbm, rows_hbm, cols_hbm, count_hbm, tiles_hbm, left_hbm, right_hbm, slip, misfit,
    data, source, tiles, far_left, far_right, near_rows, near_cols, near_count, table, table_s, halo, onehot, g,
    pc_send, pc_recv, px_send, px_recv, q_send, q_recv, v, f_send, f_recv, f_all, left, alphas, betas, inverse,
    previous, coef, sa_send, sa_recv, sb_send, sb_recv, sz_send, sz_recv, in_sem, halo_ss, halo_rs, c_ss, c_rs,
    x_ss, x_rs, y_ss, y_rs, yg_ss, yg_rs, xg_ss, xg_rs, cg_ss, cg_rs, z_ss, z_rs, zg_ss, zg_rs, sa_ss, sa_rs,
    sb_ss, sb_rs, sz_ss, sz_rs,
):
    place = lax.axis_index("rows")
    z = lax.axis_index("cols")
    core = lax.rem(place, 2)
    chip = place // 2
    y = lax.rem(chip, s.ny)
    x = chip // s.ny
    other = 1 - core
    own_q = core * s.nx + x
    n = s.realiz

    def at(xx, yy, cc):
        return ((xx * s.ny + yy) * 2 + cc, z)

    def cross(d):
        q = lax.rem(own_q + d, s.nq)
        return at(lax.rem(q, s.nx), y, q // s.nx)

    def beside(d):
        return lax.rem(x + d + s.nx, s.nx)

    mate = at(x, y, other)
    crosses = [None] + [cross(d) for d in range(1, s.nq)]
    in_x = [None] + [at(beside(d), y, core) for d in range(1, s.nx)]
    y_of = [lax.rem(y + d, s.ny) for d in range(s.ny)]
    in_y = [None] + [at(x, y_of[d], core) for d in range(1, s.ny)]
    z_of = [lax.rem(z + d, s.nz) for d in range(s.nz)]
    in_z = [None] + [(place, z_of[d]) for d in range(1, s.nz)]
    to_q = [[cc * s.nx + beside(d) for d in range(s.nx)] for cc in (core, other)]
    from_q = [[cc * s.nx + beside(-d) for d in range(s.nx)] for cc in (core, other)]

    def send(src, dst, send_sem, recv_sem, device):
        pltpu.make_async_remote_copy(
            src_ref=src, dst_ref=dst, send_sem=send_sem, recv_sem=recv_sem, device_id=device, device_id_type=MESH
        ).start()

    pairs = [
        (rows_hbm, near_rows),
        (cols_hbm, near_cols),
        (count_hbm, near_count),
        (source_hbm, source),
        (data_hbm, data),
        (left_hbm, far_left),
        (right_hbm, far_right),
        (tiles_hbm, tiles),
    ]
    loads = [pltpu.make_async_copy(src, dst, in_sem.at[k]) for k, (src, dst) in enumerate(pairs)]
    for load in loads:
        load.start()

    step_out = lax.rem(place + s.rows + 2 * core - 1, s.rows)
    partners = crosses[1:] + in_y[1:] + in_z[1:]
    partners += [(step_out, z)]
    barrier = pltpu.get_barrier_semaphore()
    for device in partners:
        pl.semaphore_signal(barrier, inc=1, device_id=device, device_id_type=MESH)

    for load in loads[:3]:
        load.wait()
    per_row = s.width // s.tile_cols
    spot = lax.broadcasted_iota(jnp.int32, (8, LANE), 1)
    slot_of = jnp.full((8, LANE), -1, jnp.int32)
    for k in range(s.slots):
        where = jnp.where(k < near_count[0, 0], near_rows[k] * per_row + near_cols[k], -1)
        slot_of = jnp.where(spot == where, k, slot_of)
    table[...] = slot_of
    to_scalars = pltpu.make_async_copy(table, table_s, in_sem.at[8])
    to_scalars.start()

    pl.semaphore_wait(barrier, len(partners))

    after = lax.rem(place + 1, s.rows)
    before = lax.rem(place + s.rows - 1, s.rows)
    loads[4].wait()
    send(data, halo.at[0], halo_ss.at[0], halo_rs.at[0], (after, z))
    send(data, halo.at[1], halo_ss.at[0], halo_rs.at[1], (before, z))

    loads[3].wait()
    total = s.rows * s.pixels
    offset = source[...] + s.pixels - place * s.pixels
    offset = jnp.where(offset < 0, offset + total, offset)
    offset = jnp.where(offset >= total, offset - total, offset)
    index = lax.broadcasted_iota(jnp.int32, (s.pixels, s.pixels), 0)
    for k in range(3):
        onehot[k] = jnp.where(index == offset - k * s.pixels, 1.0, 0.0).astype(BF16)

    for load in loads[5:]:
        load.wait()
    to_scalars.wait()
    half = per_row // 2
    half_blocks = half * s.tile_cols // LANE
    bands = s.pixels // s.tile_rows

    def build(i, carry):
        side, a = i // bands, lax.rem(i, bands)
        pixel = pl.ds(pl.multiple_of(a * s.tile_rows, s.tile_rows), s.tile_rows)
        lefts = far_left[:, pixel]
        for b in range(half):
            column = pl.ds(pl.multiple_of((side * half + b) * s.tile_cols, s.tile_cols), s.tile_cols)
            block = lax.dot_general(lefts, far_right[:, column], (((0,), (0,)), ((), ())), preferred_element_type=F32)
            slot = table_s[0, a * per_row + side * half + b]
            near = tiles[jnp.maximum(slot, 0)].astype(F32)
            block = (block + near * jnp.where(slot >= 0, 1.0, 0.0)).astype(BF16)
            for k in range(s.tile_cols // LANE):
                j = b * (s.tile_cols // LANE) + k
                q = side * (half_blocks // s.nb) + j // s.nb
                lane = (j % s.nb) * LANE
                g[q, pixel, lane : lane + LANE] = block[:, k * LANE : (k + 1) * LANE]
        return carry

    lax.fori_loop(0, 2 * bands, build, 0)

    seen = jnp.dot(three_parts(data[...]), onehot[1], preferred_element_type=F32)
    for k in range(2):
        await_bytes(halo.at[k], halo_rs.at[k])
        seen = seen + jnp.dot(three_parts(halo[k]), onehot[2 * k], preferred_element_type=F32)
    observed = (seen[0:n] + seen[n : 2 * n]) + seen[2 * n : 3 * n]
    misfit[...] = observed
    left[...] = observed
    previous[...] = jnp.zeros_like(previous)
    inverse[...] = jnp.zeros_like(inverse)

    def sum_start(i, column):
        sa_send[i] = to_row(column)
        for d in range(1, s.nq):
            send(sa_send.at[i], sa_recv.at[i, d - 1], sa_ss.at[i], sa_rs.at[i], crosses[d])

    def sum_middle(i):
        await_bytes(sa_recv.at[i], sa_rs.at[i])
        sb_send[i] = sa_send[i] + jnp.sum(sa_recv[i], axis=0)
        for d in range(1, s.ny):
            send(sb_send.at[i], sb_recv.at[i, d - 1], sb_ss.at[i], sb_rs.at[i], in_y[d])

    def sum_end(i):
        await_bytes(sb_recv.at[i], sb_rs.at[i])
        return jnp.sqrt(from_row(sb_send[i] + jnp.sum(sb_recv[i], axis=0), n) + EPSILON)

    def square_sums(it):
        def squares(q, running):
            for p, part in enumerate(s.parts):
                for j in range(part.blocks):
                    block = v[it, q, p, j * s.groups : (j + 1) * s.groups].astype(F32).reshape(n, LANE)
                    running = running + block * block
            return running

        running = lax.fori_loop(0, s.nq, squares, jnp.zeros((n, LANE), F32))
        return jnp.sum(running, axis=1, keepdims=True)

    def predicted(it, j):
        return f_all[it, j * s.groups : (j + 1) * s.groups].astype(F32).reshape(n, LANE)

    def left_sums():
        return row_sums(lane_blocks(left[...]))

    def iteration(it, carry):
        pixel_b = left[...].astype(BF16)

        def product(p, q):
            return as_tiles(jnp.dot(pixel_b, g[q, :, s.parts[p].lanes], preferred_element_type=F32))

        def to_mate(p, d):
            tb = s.parts[p].tb
            mine = pc_send.at[it, p, d, 0:tb]
            mine[...] = product(p, to_q[1][d]).astype(BF16)
            send(mine, pc_recv.at[it, p, d, 0:tb], c_ss.at[it, p], c_rs.at[it, p, d], mate)

        def pair_sum(p, d):
            own = product(p, to_q[0][d])
            came = pc_recv.at[it, p, d, 0 : s.parts[p].tb]
            await_bytes(came, c_rs.at[it, p, d])
            return own + came[...].astype(F32)

        def scatter_x(p, d):
            mine = px_send.at[it, p, d - 1, 0 : s.parts[p].tb]
            mine[...] = pair_sum(p, d).astype(BF16)
            send(mine, px_recv.at[it, p, d - 1, 0 : s.parts[p].tb], x_ss.at[it, p], x_rs.at[it, p, d - 1], in_x[d])

        def scatter_y(p):
            tb, tp, tq = s.parts[p].tb, s.parts[p].tp, s.parts[p].tq
            own = pair_sum(p, 0)
            for d in near_first(s.nx):
                came = px_recv.at[it, p, d - 1, 0:tb]
                await_bytes(came, x_rs.at[it, p, d - 1])
                own = own + came[...].astype(F32)
            q_send[it, p, 0:tb] = own.astype(BF16)
            if tq > tb:
                q_send[it, p, tb:tq] = jnp.zeros((tq - tb, TILE, LANE), BF16)
            for d in far_first(s.ny):
                piece = q_send.at[it, p, pl.ds(y_of[d] * tp, tp)]
                send(piece, q_recv.at[it, p, d - 1, 0:tp], y_ss.at[it, p], y_rs.at[it, p], in_y[d])

        def spread_y(p):
            tp = s.parts[p].tp
            await_bytes(q_recv.at[it, p, :, 0:tp], y_rs.at[it, p])
            share = q_send[it, p, pl.ds(y * tp, tp)].astype(F32)
            for d in range(s.ny - 1):
                share = share + q_recv[it, p, d, 0:tp].astype(F32)
            mine = v.at[it, own_q, p, pl.ds(y * tp, tp)]
            for i in range(tp):
                group = lax.rem(y * tp + i, s.groups)
                raw = share[i] * coef[0, group] - previous[p, i] * coef[1, group]
                previous[p, i] = raw
                v[it, own_q, p, y * tp + i] = raw.astype(BF16)
            for d in far_first(s.ny):
                send(mine, mine, yg_ss.at[it, p], yg_rs.at[it, p], in_y[d])

        def applied(p, q):
            return lax.dot_general(
                from_tiles(v[it, q, p, 0 : s.parts[p].tb], s.groups),
                g[q, :, s.parts[p].lanes],
                (((1,), (1,)), ((), ())),
                preferred_element_type=F32,
            )

        order = far_first(s.nx)
        for d in order:
            to_mate(0, d)
        for d in order:
            scatter_x(0, d)
        sum_start(it, left_sums())
        to_mate(0, 0)
        for d in order:
            to_mate(1, d)
        for d in order:
            scatter_x(1, d)
        sum_middle(it)
        scatter_y(0)
        to_mate(1, 0)
        scatter_y(1)
        beta = sum_end(it)
        betas[it] = beta
        coef[0] = (1.0 / beta).reshape(s.groups, TILE, LANE)
        coef[1] = (beta * inverse[...]).reshape(s.groups, TILE, LANE)
        for p in range(2):
            spread_y(p)

        total = jnp.zeros((n, s.pixels), F32)
        for p, part in enumerate(s.parts):
            await_bytes(q_recv.at[it, p, :, 0 : part.tp], yg_rs.at[it, p])
            ready = v.at[it, own_q, p, 0 : part.tb]
            for d in far_first(s.nx):
                send(ready, ready, xg_ss.at[it, p], xg_rs.at[it, p, d - 1], in_x[d])
            send(ready, ready, cg_ss.at[it, p], cg_rs.at[it, p, 0], mate)
            total = total + applied(p, own_q)
        for p, part in enumerate(s.parts):
            for d in near_first(s.nx):
                q = from_q[0][d]
                came = v.at[it, q, p, 0 : part.tb]
                await_bytes(came, xg_rs.at[it, p, d - 1])
                send(came, came, cg_ss.at[it, p], cg_rs.at[it, p, d], mate)
                total = total + applied(p, q)
            for d in [0] + near_first(s.nx):
                q = from_q[1][d]
                await_bytes(v.at[it, q, p, 0 : part.tb], cg_rs.at[it, p, d])
                total = total + applied(p, q)

        f_send[it, 0 : s.ft] = as_tiles(total).astype(BF16)
        if s.fz > s.ft:
            f_send[it, s.ft : s.fz] = jnp.zeros((s.fz - s.ft, TILE, LANE), BF16)
        for d in far_first(s.nz):
            piece = f_send.at[it, pl.ds(z_of[d] * s.zp, s.zp)]
            send(piece, f_recv.at[it, d - 1], z_ss.at[it], z_rs.at[it], in_z[d])
        sz_send[it] = to_row(square_sums(it))
        for d in far_first(s.nz):
            send(sz_send.at[it], sz_recv.at[it, d - 1], sz_ss.at[it], sz_rs.at[it], in_z[d])
        await_bytes(f_recv.at[it], z_rs.at[it])
        reduced = f_send[it, pl.ds(z * s.zp, s.zp)].astype(F32)
        for d in range(s.nz - 1):
            reduced = reduced + f_recv[it, d].astype(F32)
        mine = f_all.at[it, pl.ds(z * s.zp, s.zp)]
        mine[...] = reduced.astype(BF16)
        for d in far_first(s.nz):
            send(mine, mine, zg_ss.at[it], zg_rs.at[it], in_z[d])
        await_bytes(sz_recv.at[it], sz_rs.at[it])
        alpha = jnp.sqrt(from_row(sz_send[it] + jnp.sum(sz_recv[it], axis=0), n) + EPSILON)
        alphas[it] = alpha
        inverse[...] = 1.0 / alpha
        ratio = alpha / beta
        await_bytes(f_recv.at[it], zg_rs.at[it])
        for j in range(s.fb):
            lanes = slice(j * LANE, (j + 1) * LANE)
            left[:, lanes] = predicted(it, j) * inverse[...] - left[:, lanes] * ratio
        return carry

    lax.fori_loop(0, 2, iteration, 0)

    sum_start(2, left_sums())
    alpha1, alpha2, beta1, beta2 = alphas[0], alphas[1], betas[0], betas[1]
    rho1 = jnp.sqrt(alpha1 * alpha1 + beta2 * beta2)
    cosine, sine = alpha1 / rho1, beta2 / rho1
    phi1 = cosine * beta1
    phibar = sine * beta1
    theta = sine * alpha2
    rhobar = -cosine * alpha2

    first = place * (s.width // s.rows)
    block = first // LANE
    lane = lax.rem(first, LANE)
    share_width = s.width // s.rows
    cover = -(-share_width // LANE)
    shape = ((cover + 1) * LANE, cover * LANE)
    pick = lax.broadcasted_iota(jnp.int32, shape, 0) == lax.broadcasted_iota(jnp.int32, shape, 1) + lane
    pick = jnp.where(pick, 1.0, 0.0).astype(BF16)
    window = []
    for it in range(2):
        sides = []
        for k in range(cover + 1):
            b = jnp.minimum(block + k, s.width // LANE - 1)
            j = lax.rem(b, s.nb)
            p = j // s.cut
            inside = (j - p * s.cut) * s.groups
            sides.append(v[it, b // s.nb, p, pl.ds(inside, s.groups)].reshape(n, LANE))
        window.append(jnp.dot(jnp.concatenate(sides, axis=1), pick, preferred_element_type=F32))

    sum_middle(2)
    beta3 = sum_end(2)
    rho2 = jnp.sqrt(rhobar * rhobar + beta3 * beta3)
    phi2 = rhobar / rho2 * phibar
    on2 = phi2 / rho2
    weight1 = (phi1 / rho1 - on2 * (theta / rho1)) / alpha1
    weight2 = on2 / alpha2
    result = [weight1 * a + weight2 * b for a, b in zip(lane_blocks(window[0]), lane_blocks(window[1]), strict=True)]
    slip[...] = jnp.concatenate(result, axis=1)[:, 0:share_width]
    for j in range(s.fb):
        lanes = slice(j * LANE, (j + 1) * LANE)
        misfit[:, lanes] = misfit[:, lanes] - weight1 * predicted(0, j) - weight2 * predicted(1, j)

    await_bytes(halo, halo_ss.at[0])

    def settle(it, carry):
        for p, part in enumerate(s.parts):
            four = pc_send.at[it, p, :, 0 : part.tb]
            three = px_send.at[it, p, :, 0 : part.tb]
            pieces = q_recv.at[it, p, :, 0 : part.tp]
            await_bytes(four, c_ss.at[it, p])
            await_bytes(three, x_ss.at[it, p])
            await_bytes(pieces, y_ss.at[it, p])
            await_bytes(pieces, yg_ss.at[it, p])
            await_bytes(three, xg_ss.at[it, p])
            await_bytes(four, cg_ss.at[it, p])
        await_bytes(f_recv.at[it], z_ss.at[it])
        await_bytes(f_recv.at[it], zg_ss.at[it])
        await_bytes(sz_recv.at[it], sz_ss.at[it])
        return carry

    lax.fori_loop(0, 2, settle, 0)
    for i in range(3):
        await_bytes(sa_recv.at[i], sa_ss.at[i])
        await_bytes(sb_recv.at[i], sb_ss.at[i])


def body(dims, nz, data, source, near_tiles, near_rows, near_cols, near_count, far_left, far_right):
    realiz, pixels = data.shape
    rank, width = far_right.shape
    slots, tile_rows, tile_cols = near_tiles.shape
    s = Sizes(dims, nz, realiz, pixels, width, slots, rank, tile_rows, tile_cols)
    vmem = pl.BlockSpec(memory_space=pltpu.VMEM)
    pin = functools.partial(pltpu.with_memory_space_constraint, memory_space=pltpu.HBM)
    return pl.pallas_call(
        functools.partial(kernel, s),
        out_shape=(pltpu.VMEM((realiz, width // s.rows), F32), pltpu.VMEM((realiz, pixels), F32)),
        in_specs=[pl.BlockSpec(memory_space=pl.ANY)] * 8,
        out_specs=(vmem, vmem),
        scratch_shapes=scratch_shapes(s),
        compiler_params=pltpu.CompilerParams(
            collective_id=0, has_side_effects=True, vmem_limit_bytes=48 * 1024 * 1024
        ),
    )(
        pin(data),
        pin(source.reshape(1, pixels)),
        pin(near_rows.reshape(slots)),
        pin(near_cols.reshape(slots)),
        near_count,
        pin(near_tiles),
        pin(far_left),
        pin(far_right),
    )


def solution(mesh, dims=(4, 8, 2)):
    return jax.shard_map(
        functools.partial(body, dims, mesh.shape["cols"]),
        mesh=mesh,
        in_specs=(
            P(None, "rows"),
            P("rows"),
            P("rows", "cols", None),
            P("rows", "cols"),
            P("rows", "cols"),
            P("rows", "cols"),
            P("cols", "rows"),
            P("rows", "cols"),
        ),
        out_specs=(P(None, ("cols", "rows")), P(None, "rows")),
        check_vma=False,
    )
```

time: 109 us -> 101 us (0.927)
  Pallas kernels: 105 us -> 98.2 us
  local copies, waits for them, and re-layouts: 2.99 us -> 1.29 us
    pallas_call x1, Pallas kernels: 105 us -> 98.2 us  [body(): pl.pallas_call(functools.partial(kernel, s), out_shape=(pltpu.VMEM((reali...]
    unnamed x2, local copies, waits for them, and re-layouts: 2.99 us -> 1.29 us
where the time goes in v4:
time: 101 us
  Pallas kernels  98.2 us (97%)
  local copies, waits for them, and re-layouts  1.29 us (1%)
  between operations  1.29 us (1%)
    pallas_call x1, Pallas kernels, body(): pl.pallas_call(functools.partial(kernel, s), out_shape=(pltpu.VMEM((reali...  98.2 us

profile of v4, /device:TPU:1, one launch (start us, length us, event | category | flops | bytes accessed | tf_op | source)
XLA Modules:
  0.0 100.8 jit_solution(11656992435801926462)
XLA Ops:
  1.3 98.2 %shard_map.95 = (f32[80,80]{1,0:T(8,128)S(1)}, f32[80,512]{1,0:T(8,128)S(1)}) custom-call(f32[80,512]{1,0:T(8,128)} %data_hbm.1, s32[1,512]{1,0:T(1,128)} %bitcast.3, s32[30]{0:T(128)} %bitcast.4, s32[30]{0:T(128)} %bitcast.5, s32[1,1]{1,0:T(1,128)S(6)} %copy.14.count_hbm, bf16[30,128,512]{2,1,0:T(8,128)(2,1)} %tiles_hbm.1, bf16[24,512]{1,0:T(8,128)(2,1)} %left_hbm.1, ...), custom_call_target="tpu_custom_call" | custom-call | tf_op jit(solution)/shard_map/pallas_call | solution.py:535
  99.5 0.6 copy.12
  100.1 0.7 copy.13

commit v5 on v4

--- a/solution.py
+++ b/solution.py
@@ -22,6 +22,8 @@
         self.tb = blocks * s.groups
         self.tp = -(-self.tb // s.ny)
         self.tq = self.tp * s.ny
+        half = (self.tb + 1) // 2
+        self.halves = ((0, half), (half, self.tb))
 
 
 class Sizes:
@@ -52,7 +54,7 @@
     return [
         pltpu.VMEM((s.realiz, s.pixels), F32),
         pltpu.VMEM((1, s.pixels), jnp.int32),
-        pltpu.VMEM((s.slots, s.tile_rows, s.tile_cols), BF16),
+        pltpu.VMEM((s.slots + 1, s.tile_rows, s.tile_cols), BF16),
         pltpu.VMEM((s.rank, s.pixels), BF16),
         pltpu.VMEM((s.rank, s.width), BF16),
         pltpu.SMEM((s.slots,), jnp.int32),
@@ -97,9 +99,9 @@
         dma((2, 2)),
         dma((2, 2)),
         dma((2, 2)),
-        dma((2, 2, s.nx - 1)),
-        dma((2, 2)),
-        dma((2, 2, s.nx)),
+        dma((2, 2, 4)),
+        dma((2, 2)),
+        dma((2, 2, 5)),
         dma((2,)),
         dma((2,)),
         dma((2,)),
@@ -218,7 +220,7 @@
         (data_hbm, data),
         (left_hbm, far_left),
         (right_hbm, far_right),
-        (tiles_hbm, tiles),
+        (tiles_hbm, tiles.at[0 : s.slots]),
     ]
     loads = [pltpu.make_async_copy(src, dst, in_sem.at[k]) for k, (src, dst) in enumerate(pairs)]
     for load in loads:
@@ -231,11 +233,12 @@
     for device in partners:
         pl.semaphore_signal(barrier, inc=1, device_id=device, device_id_type=MESH)
 
+    tiles[s.slots] = jnp.zeros((s.tile_rows, s.tile_cols), BF16)
     for load in loads[:3]:
         load.wait()
     per_row = s.width // s.tile_cols
     spot = lax.broadcasted_iota(jnp.int32, (8, LANE), 1)
-    slot_of = jnp.full((8, LANE), -1, jnp.int32)
+    slot_of = jnp.full((8, LANE), s.slots, jnp.int32)
     for k in range(s.slots):
         where = jnp.where(k < near_count[0, 0], near_rows[k] * per_row + near_cols[k], -1)
         slot_of = jnp.where(spot == where, k, slot_of)
@@ -274,9 +277,8 @@
         for b in range(half):
             column = pl.ds(pl.multiple_of((side * half + b) * s.tile_cols, s.tile_cols), s.tile_cols)
             block = lax.dot_general(lefts, far_right[:, column], (((0,), (0,)), ((), ())), preferred_element_type=F32)
-            slot = table_s[0, a * per_row + side * half + b]
-            near = tiles[jnp.maximum(slot, 0)].astype(F32)
-            block = (block + near * jnp.where(slot >= 0, 1.0, 0.0)).astype(BF16)
+            near = tiles[table_s[0, a * per_row + side * half + b]]
+            block = (block + near.astype(F32)).astype(BF16)
             for k in range(s.tile_cols // LANE):
                 j = b * (s.tile_cols // LANE) + k
                 q = side * (half_blocks // s.nb) + j // s.nb
@@ -414,21 +416,37 @@
         for p, part in enumerate(s.parts):
             await_bytes(q_recv.at[it, p, :, 0 : part.tp], yg_rs.at[it, p])
             ready = v.at[it, own_q, p, 0 : part.tb]
-            for d in far_first(s.nx):
-                send(ready, ready, xg_ss.at[it, p], xg_rs.at[it, p, d - 1], in_x[d])
+            for k, device in enumerate((in_x[1], in_x[-1])):
+                send(ready, ready, xg_ss.at[it, p], xg_rs.at[it, p, k], device)
             send(ready, ready, cg_ss.at[it, p], cg_rs.at[it, p, 0], mate)
             total = total + applied(p, own_q)
         for p, part in enumerate(s.parts):
-            for d in near_first(s.nx):
+            for k, d in enumerate((1, -1)):
                 q = from_q[0][d]
                 came = v.at[it, q, p, 0 : part.tb]
-                await_bytes(came, xg_rs.at[it, p, d - 1])
-                send(came, came, cg_ss.at[it, p], cg_rs.at[it, p, d], mate)
+                await_bytes(came, xg_rs.at[it, p, k])
+                lo, hi = part.halves[k]
+                onward = v.at[it, q, p, lo:hi]
+                send(onward, onward, xg_ss.at[it, p], xg_rs.at[it, p, 2 + k], in_x[d])
+                send(came, came, cg_ss.at[it, p], cg_rs.at[it, p, 1 + k], mate)
+            total = total + applied(p, from_q[0][1])
+            total = total + applied(p, from_q[0][-1])
+        for p, part in enumerate(s.parts):
+            q = from_q[0][2]
+            for k, (lo, hi) in enumerate(part.halves):
+                came = v.at[it, q, p, lo:hi]
+                await_bytes(came, xg_rs.at[it, p, 2 + k])
+                send(came, came, cg_ss.at[it, p], cg_rs.at[it, p, 3 + k], mate)
+            total = total + applied(p, q)
+            for k, d in enumerate((0, 1, -1)):
+                q = from_q[1][d]
+                await_bytes(v.at[it, q, p, 0 : part.tb], cg_rs.at[it, p, k])
                 total = total + applied(p, q)
-            for d in [0] + near_first(s.nx):
-                q = from_q[1][d]
-                await_bytes(v.at[it, q, p, 0 : part.tb], cg_rs.at[it, p, d])
-                total = total + applied(p, q)
+        for p, part in enumerate(s.parts):
+            q = from_q[1][2]
+            for k, (lo, hi) in enumerate(part.halves):
+                await_bytes(v.at[it, q, p, lo:hi], cg_rs.at[it, p, 3 + k])
+            total = total + applied(p, q)
 
         f_send[it, 0 : s.ft] = as_tiles(total).astype(BF16)
         if s.fz > s.ft:

time: 101 us -> 106 us (1.050)
  Pallas kernels: 98.2 us -> 103 us
    pallas_call x1, Pallas kernels: 98.2 us -> 103 us  [body(): pl.pallas_call(functools.partial(kernel, s), out_shape=(pltpu.VMEM((reali...]
where the time goes in v5:
time: 106 us
  Pallas kernels  103 us (97%)
  local copies, waits for them, and re-layouts  1.29 us (1%)
  between operations  1.29 us (1%)
    pallas_call x1, Pallas kernels, body(): pl.pallas_call(functools.partial(kernel, s), out_shape=(pltpu.VMEM((reali...  103 us

profile of v5, /device:TPU:1, one launch (start us, length us, event | category | flops | bytes accessed | tf_op | source)
XLA Modules:
  0.0 105.8 jit_solution(11729545262404298573)
XLA Ops:
  1.3 103.2 %shard_map.95 = (f32[80,80]{1,0:T(8,128)S(1)}, f32[80,512]{1,0:T(8,128)S(1)}) custom-call(f32[80,512]{1,0:T(8,128)} %data_hbm.1, s32[1,512]{1,0:T(1,128)} %bitcast.3, s32[30]{0:T(128)} %bitcast.4, s32[30]{0:T(128)} %bitcast.5, s32[1,1]{1,0:T(1,128)S(6)} %copy.14.count_hbm, bf16[30,128,512]{2,1,0:T(8,128)(2,1)} %tiles_hbm.1, bf16[24,512]{1,0:T(8,128)(2,1)} %left_hbm.1, ...), custom_call_target="tpu_custom_call" | custom-call | tf_op jit(solution)/shard_map/pallas_call | solution.py:553
  104.5 0.6 copy.12
  105.1 0.7 copy.13

commit v6 on v4

--- a/solution.py
+++ b/solution.py
@@ -52,7 +52,7 @@
     return [
         pltpu.VMEM((s.realiz, s.pixels), F32),
         pltpu.VMEM((1, s.pixels), jnp.int32),
-        pltpu.VMEM((s.slots, s.tile_rows, s.tile_cols), BF16),
+        pltpu.VMEM((s.slots + 1, s.tile_rows, s.tile_cols), BF16),
         pltpu.VMEM((s.rank, s.pixels), BF16),
         pltpu.VMEM((s.rank, s.width), BF16),
         pltpu.SMEM((s.slots,), jnp.int32),
@@ -210,6 +210,13 @@
             src_ref=src, dst_ref=dst, send_sem=send_sem, recv_sem=recv_sem, device_id=device, device_id_type=MESH
         ).start()
 
+    step_out = lax.rem(place + s.rows + 2 * core - 1, s.rows)
+    partners = crosses[1:] + in_y[1:] + in_z[1:]
+    partners += [(step_out, z)]
+    barrier = pltpu.get_barrier_semaphore()
+    for device in partners:
+        pl.semaphore_signal(barrier, inc=1, device_id=device, device_id_type=MESH)
+
     pairs = [
         (rows_hbm, near_rows),
         (cols_hbm, near_cols),
@@ -218,38 +225,31 @@
         (data_hbm, data),
         (left_hbm, far_left),
         (right_hbm, far_right),
-        (tiles_hbm, tiles),
+        (tiles_hbm, tiles.at[0 : s.slots]),
     ]
     loads = [pltpu.make_async_copy(src, dst, in_sem.at[k]) for k, (src, dst) in enumerate(pairs)]
     for load in loads:
         load.start()
 
-    step_out = lax.rem(place + s.rows + 2 * core - 1, s.rows)
-    partners = crosses[1:] + in_y[1:] + in_z[1:]
-    partners += [(step_out, z)]
-    barrier = pltpu.get_barrier_semaphore()
-    for device in partners:
-        pl.semaphore_signal(barrier, inc=1, device_id=device, device_id_type=MESH)
-
+    pl.semaphore_wait(barrier, len(partners))
+
+    after = lax.rem(place + 1, s.rows)
+    before = lax.rem(place + s.rows - 1, s.rows)
+    send(data_hbm, halo.at[0], halo_ss.at[0], halo_rs.at[0], (after, z))
+    send(data_hbm, halo.at[1], halo_ss.at[0], halo_rs.at[1], (before, z))
+
+    tiles[s.slots] = jnp.zeros((s.tile_rows, s.tile_cols), BF16)
     for load in loads[:3]:
         load.wait()
     per_row = s.width // s.tile_cols
     spot = lax.broadcasted_iota(jnp.int32, (8, LANE), 1)
-    slot_of = jnp.full((8, LANE), -1, jnp.int32)
+    slot_of = jnp.full((8, LANE), s.slots, jnp.int32)
     for k in range(s.slots):
         where = jnp.where(k < near_count[0, 0], near_rows[k] * per_row + near_cols[k], -1)
         slot_of = jnp.where(spot == where, k, slot_of)
     table[...] = slot_of
     to_scalars = pltpu.make_async_copy(table, table_s, in_sem.at[8])
     to_scalars.start()
-
-    pl.semaphore_wait(barrier, len(partners))
-
-    after = lax.rem(place + 1, s.rows)
-    before = lax.rem(place + s.rows - 1, s.rows)
-    loads[4].wait()
-    send(data, halo.at[0], halo_ss.at[0], halo_rs.at[0], (after, z))
-    send(data, halo.at[1], halo_ss.at[0], halo_rs.at[1], (before, z))
 
     loads[3].wait()
     total = s.rows * s.pixels
@@ -260,7 +260,7 @@
     for k in range(3):
         onehot[k] = jnp.where(index == offset - k * s.pixels, 1.0, 0.0).astype(BF16)
 
-    for load in loads[5:]:
+    for load in loads[4:]:
         load.wait()
     to_scalars.wait()
     half = per_row // 2
@@ -274,9 +274,8 @@
         for b in range(half):
             column = pl.ds(pl.multiple_of((side * half + b) * s.tile_cols, s.tile_cols), s.tile_cols)
             block = lax.dot_general(lefts, far_right[:, column], (((0,), (0,)), ((), ())), preferred_element_type=F32)
-            slot = table_s[0, a * per_row + side * half + b]
-            near = tiles[jnp.maximum(slot, 0)].astype(F32)
-            block = (block + near * jnp.where(slot >= 0, 1.0, 0.0)).astype(BF16)
+            near = tiles[table_s[0, a * per_row + side * half + b]]
+            block = (block + near.astype(F32)).astype(BF16)
             for k in range(s.tile_cols // LANE):
                 j = b * (s.tile_cols // LANE) + k
                 q = side * (half_blocks // s.nb) + j // s.nb
@@ -391,17 +390,16 @@
         order = far_first(s.nx)
         for d in order:
             to_mate(0, d)
-        for d in order:
-            scatter_x(0, d)
         sum_start(it, left_sums())
-        to_mate(0, 0)
         for d in order:
             to_mate(1, d)
+            scatter_x(0, d)
+        to_mate(0, 0)
+        to_mate(1, 0)
         for d in order:
             scatter_x(1, d)
+        scatter_y(0)
         sum_middle(it)
-        scatter_y(0)
-        to_mate(1, 0)
         scatter_y(1)
         beta = sum_end(it)
         betas[it] = beta
@@ -425,6 +423,7 @@
                 await_bytes(came, xg_rs.at[it, p, d - 1])
                 send(came, came, cg_ss.at[it, p], cg_rs.at[it, p, d], mate)
                 total = total + applied(p, q)
+        for p, part in enumerate(s.parts):
             for d in [0] + near_first(s.nx):
                 q = from_q[1][d]
                 await_bytes(v.at[it, q, p, 0 : part.tb], cg_rs.at[it, p, d])

time: 101 us -> 101 us (level)
  no operation moved by 1% of the time
where the time goes in v6:
time: 101 us
  Pallas kernels  98.6 us (98%)
  local copies, waits for them, and re-layouts  1.29 us (1%)
  between operations  1.29 us (1%)
    pallas_call x1, Pallas kernels, body(): pl.pallas_call(functools.partial(kernel, s), out_shape=(pltpu.VMEM((reali...  98.6 us

profile of v6, /device:TPU:1, one launch (start us, length us, event | category | flops | bytes accessed | tf_op | source)
XLA Modules:
  0.0 101.2 jit_solution(2488277986253476536)
XLA Ops:
  1.3 98.6 %shard_map.95 = (f32[80,80]{1,0:T(8,128)S(1)}, f32[80,512]{1,0:T(8,128)S(1)}) custom-call(f32[80,512]{1,0:T(8,128)} %data_hbm.1, s32[1,512]{1,0:T(1,128)} %bitcast.3, s32[30]{0:T(128)} %bitcast.4, s32[30]{0:T(128)} %bitcast.5, s32[1,1]{1,0:T(1,128)S(6)} %copy.14.count_hbm, bf16[30,128,512]{2,1,0:T(8,128)(2,1)} %tiles_hbm.1, bf16[24,512]{1,0:T(8,128)(2,1)} %left_hbm.1, ...), custom_call_target="tpu_custom_call" | custom-call | tf_op jit(solution)/shard_map/pallas_call | solution.py:534
  99.9 0.6 copy.12
  100.5 0.7 copy.13

commit v7 on v6

--- a/solution.py
+++ b/solution.py
@@ -39,8 +39,8 @@
         self.ft = self.fb * self.groups
         self.zp = -(-self.ft // nz)
         self.fz = self.zp * nz
-        self.cut = (self.nb + 1) // 2
-        self.parts = [Part(0, self.cut, self), Part(self.cut, self.nb - self.cut, self)]
+        self.cut = self.nb
+        self.parts = [Part(0, self.nb, self)]
         self.tb = max(p.tb for p in self.parts)
         self.tp = max(p.tp for p in self.parts)
         self.tq = max(p.tq for p in self.parts)
@@ -63,13 +63,13 @@
         pltpu.VMEM((2, s.realiz, s.pixels), F32),
         pltpu.VMEM((3, s.pixels, s.pixels), BF16),
         pltpu.VMEM((s.nq, s.pixels, s.chunk), BF16),
-        pltpu.VMEM((2, 2, s.nx, s.tb, *tile), BF16),
-        pltpu.VMEM((2, 2, s.nx, s.tb, *tile), BF16),
-        pltpu.VMEM((2, 2, s.nx - 1, s.tb, *tile), BF16),
-        pltpu.VMEM((2, 2, s.nx - 1, s.tb, *tile), BF16),
-        pltpu.VMEM((2, 2, s.tq, *tile), BF16),
-        pltpu.VMEM((2, 2, s.ny - 1, s.tp, *tile), BF16),
-        pltpu.VMEM((2, s.nq, 2, s.tq, *tile), BF16),
+        pltpu.VMEM((2, len(s.parts), s.nx, s.tb, *tile), BF16),
+        pltpu.VMEM((2, len(s.parts), s.nx, s.tb, *tile), BF16),
+        pltpu.VMEM((2, len(s.parts), s.nx - 1, s.tb, *tile), BF16),
+        pltpu.VMEM((2, len(s.parts), s.nx - 1, s.tb, *tile), BF16),
+        pltpu.VMEM((2, len(s.parts), s.tq, *tile), BF16),
+        pltpu.VMEM((2, len(s.parts), s.ny - 1, s.tp, *tile), BF16),
+        pltpu.VMEM((2, s.nq, len(s.parts), s.tq, *tile), BF16),
         pltpu.VMEM((2, s.fz, *tile), BF16),
         pltpu.VMEM((2, s.nz - 1, s.zp, *tile), BF16),
         pltpu.VMEM((2, s.fz, *tile), BF16),
@@ -77,7 +77,7 @@
         pltpu.VMEM((2, s.realiz, LANE), F32),
         pltpu.VMEM((2, s.realiz, LANE), F32),
         pltpu.VMEM((s.realiz, LANE), F32),
-        pltpu.VMEM((2, s.tp, *tile), F32),
+        pltpu.VMEM((len(s.parts), s.tp, *tile), F32),
         pltpu.VMEM((2, s.groups, *tile), F32),
         pltpu.VMEM((3, 8, LANE), F32),
         pltpu.VMEM((3, s.nq - 1, 8, LANE), F32),
@@ -89,17 +89,17 @@
         dma((1,)),
         dma((2,)),
         dma((2, 2)),
-        dma((2, 2, s.nx)),
-        dma((2, 2)),
-        dma((2, 2, s.nx - 1)),
-        dma((2, 2)),
-        dma((2, 2)),
-        dma((2, 2)),
-        dma((2, 2)),
-        dma((2, 2)),
-        dma((2, 2, s.nx - 1)),
-        dma((2, 2)),
-        dma((2, 2, s.nx)),
+        dma((2, len(s.parts), s.nx)),
+        dma((2, 2)),
+        dma((2, len(s.parts), s.nx - 1)),
+        dma((2, 2)),
+        dma((2, 2)),
+        dma((2, 2)),
+        dma((2, 2)),
+        dma((2, 2)),
+        dma((2, len(s.parts), s.nx - 1)),
+        dma((2, 2)),
+        dma((2, len(s.parts), s.nx)),
         dma((2,)),
         dma((2,)),
         dma((2,)),
@@ -388,24 +388,21 @@
             )
 
         order = far_first(s.nx)
-        for d in order:
-            to_mate(0, d)
+        for p in range(len(s.parts)):
+            for d in order:
+                to_mate(p, d)
         sum_start(it, left_sums())
-        for d in order:
-            to_mate(1, d)
-            scatter_x(0, d)
-        to_mate(0, 0)
-        to_mate(1, 0)
-        for d in order:
-            scatter_x(1, d)
-        scatter_y(0)
+        for p in range(len(s.parts)):
+            to_mate(p, 0)
+            for d in order:
+                scatter_x(p, d)
+            scatter_y(p)
         sum_middle(it)
-        scatter_y(1)
         beta = sum_end(it)
         betas[it] = beta
         coef[0] = (1.0 / beta).reshape(s.groups, TILE, LANE)
         coef[1] = (beta * inverse[...]).reshape(s.groups, TILE, LANE)
-        for p in range(2):
+        for p in range(len(s.parts)):
             spread_y(p)
 
         total = jnp.zeros((n, s.pixels), F32)

time: 101 us -> 108 us (1.069)
  Pallas kernels: 98.6 us -> 105 us
    pallas_call x1, Pallas kernels: 98.6 us -> 105 us  [body(): pl.pallas_call(functools.partial(kernel, s), out_shape=(pltpu.VMEM((reali...]
where the time goes in v7:
time: 108 us; the launch traced here: 107 us
  Pallas kernels  105 us (97%)
  local copies, waits for them, and re-layouts  1.29 us (1%)
  between operations  1.29 us (1%)
    pallas_call x1, Pallas kernels, body(): pl.pallas_call(functools.partial(kernel, s), out_shape=(pltpu.VMEM((reali...  105 us

profile of v7, /device:TPU:1, one launch (start us, length us, event | category | flops | bytes accessed | tf_op | source)
XLA Modules:
  0.0 107.4 jit_solution(7159850700771653326)
XLA Ops:
  1.3 104.8 %shard_map.95 = (f32[80,80]{1,0:T(8,128)S(1)}, f32[80,512]{1,0:T(8,128)S(1)}) custom-call(f32[80,512]{1,0:T(8,128)} %data_hbm.1, s32[1,512]{1,0:T(1,128)} %bitcast.3, s32[30]{0:T(128)} %bitcast.4, s32[30]{0:T(128)} %bitcast.5, s32[1,1]{1,0:T(1,128)S(6)} %copy.14.count_hbm, bf16[30,128,512]{2,1,0:T(8,128)(2,1)} %tiles_hbm.1, bf16[24,512]{1,0:T(8,128)(2,1)} %left_hbm.1, ...), custom_call_target="tpu_custom_call" | custom-call | tf_op jit(solution)/shard_map/pallas_call | solution.py:531
  106.1 0.6 copy.12
  106.7 0.7 copy.13
